TPU v7x, 512 devices: a whole 4x8x8 slice. The times are simulated.
512 devices in a mesh: grp: 16 (over x, y_hi), tile: 32 (over z, y_lo, core).
Axes of the slice: x: 4, y: 8 (y_hi: 4, y_lo: 2; y = y_hi * 2 + y_lo), z: 8, core: 2. Of those that a mesh axis runs over, the one named last changes fastest.
Arguments:
- base_velocity: float32 [2, 1024, 4096], P(None, 'grp', 'tile'), may hold values from -6 to 6
- viscosity: float32 [1024, 4096], P('grp', 'tile'), may hold values from 0.5 to 2
- friction: float32 [1024, 4096], P('grp', 'tile'), may hold values from 2 to 8
- friction_probe: float32 [1024, 4096], P('grp', 'tile'), may hold values from -6 to 6
- pixel_los: float32 [16, 32, 2, 2048], P('grp', 'tile'), may hold values from -6 to 6
- pixel_weight: float32 [16, 32, 1, 2048], P('grp', 'tile'), may hold values from 2 to 20
- pixel_cell: int32 [16, 32, 1, 2048], P('grp', 'tile'), may hold values from 0 to 8191
- pixel_count: int32 [16, 32, 1, 32], P('grp', 'tile'), may hold values from 8 to 64, as said below
- panels: bfloat16 [128, 1024, 4096], P('grp', None, 'tile'), may hold values from -0.00390625 to 0.00390625
Outputs:
- increment: float32 [2, 1024, 4096], P(None, 'grp', 'tile')
- hessian_probe: float32 [1024, 4096], P('grp', 'tile')
- coefficients: float32 [128], replicated
Inputs may be any that keep to these rules, and one draw needn't show every extreme that they name: In group g, tile s uses the first pixel_count[g, s, 0, o] of its 64 slots toward owner tile o; in every group some owner receives 64 from every tile, and such owners are a few times busier than the mean. `pixel_cell`: cells are numbered row by row within the owner's block of 64 x 128 cells.
All inputs are finite; a program needn't handle non-finite values.
Results may differ from a plain program's by a relative error of at most 0.0036.
Values may be sent and summed in bfloat16 or wider, within the bound.
A program may use at most 64 MiB of HBM per device.

v0:
```python
import jax
import jax.numpy as jnp
from jax import lax
from jax.sharding import PartitionSpec as P

SWEEPS = 8


relax_weight = 0.8


def with_halo(cells, sides, width):
    for axis, dim in sides:
        count = lax.axis_size(axis)
        ends = count - 1
        head = lax.slice_in_dim(cells, 0, width, axis=dim)
        tail = lax.slice_in_dim(cells, cells.shape[dim] - width, cells.shape[dim], axis=dim)
        cells = jnp.concatenate(
            [
                lax.ppermute(tail, axis, [(i, (i + 1) % count) for i in range(ends)]),
                cells,
                lax.ppermute(head, axis, [((i + 1) % count, i) for i in range(ends)]),
            ],
            axis=dim,
        )
    return cells


def face_terms(visc_ext, fric_inner):
    centre = visc_ext[1:-1, 1:-1]
    east = 0.5 * (centre + visc_ext[2:, 1:-1])
    west = 0.5 * (centre + visc_ext[:-2, 1:-1])
    north = 0.5 * (centre + visc_ext[1:-1, 2:])
    south = 0.5 * (centre + visc_ext[1:-1, :-2])
    node_pp = 0.25 * (centre + visc_ext[2:, 1:-1] + visc_ext[1:-1, 2:] + visc_ext[2:, 2:])
    node_mm = 0.25 * (centre + visc_ext[:-2, 1:-1] + visc_ext[1:-1, :-2] + visc_ext[:-2, :-2])
    node_pm = 0.25 * (centre + visc_ext[2:, 1:-1] + visc_ext[1:-1, :-2] + visc_ext[2:, :-2])
    node_mp = 0.25 * (centre + visc_ext[:-2, 1:-1] + visc_ext[1:-1, 2:] + visc_ext[:-2, 2:])
    diag_x = fric_inner + 2.0 * (east + west) + (north + south)
    diag_y = fric_inner + (east + west) + 2.0 * (north + south)
    return jnp.stack([east, west, north, south, node_pp, node_mm, node_pm, node_mp, diag_x, diag_y])


def operate(field_ext, terms):
    east, west, north, south = (terms[0], terms[1], terms[2], terms[3])
    node_pp, node_mm, node_pm, node_mp = (terms[4], terms[5], terms[6], terms[7])
    first = field_ext[0]
    second = field_ext[1]

    def axial(comp, along_one, along_two):
        return along_one * (east * comp[2:, 1:-1] + west * comp[:-2, 1:-1]) + along_two * (
            north * comp[1:-1, 2:] + south * comp[1:-1, :-2]
        )

    def cross(comp):
        return (
            node_pp * comp[2:, 2:]
            + node_mm * comp[:-2, :-2]
            - node_pm * comp[2:, :-2]
            - node_mp * comp[:-2, 2:]
        )

    out_first = terms[8] * first[1:-1, 1:-1] - axial(first, 2.0, 1.0) - 0.25 * cross(second)
    out_second = terms[9] * second[1:-1, 1:-1] - axial(second, 1.0, 2.0) - 0.25 * cross(first)
    return jnp.stack([out_first, out_second])


def on_device(
    base_velocity,
    viscosity,
    friction,
    friction_probe,
    pixel_los,
    pixel_weight,
    pixel_cell,
    pixel_count,
    panels,
):
    rows, columns = viscosity.shape
    stacked = jnp.stack([viscosity, friction])
    coarse_ext = with_halo(stacked, (("grp", 1), ("tile", 2)), 2)
    terms = face_terms(coarse_ext[0], coarse_ext[1][1:-1, 1:-1])
    row_ids = lax.axis_index("grp") * rows + jnp.arange(-1, rows + 1, dtype=jnp.int32)
    col_ids = lax.axis_index("tile") * columns + jnp.arange(-1, columns + 1, dtype=jnp.int32)
    row_inside = (row_ids >= 0) & (row_ids < rows * lax.axis_size("grp"))
    col_inside = (col_ids >= 0) & (col_ids < columns * lax.axis_size("tile"))
    inside = row_inside[:, None] & col_inside[None, :]
    diagonal = jnp.where(inside[None], terms[8:10], 1.0)

    def relax(source):
        depth = 1
        source_ext = jnp.pad(source, ((0, 0), (1, 1), (1, 1)))
        field = source
        finished = 0
        for block in range(-(-SWEEPS // depth)):
            width = min(depth, SWEEPS - finished)
            if finished == 0:
                field_ext = jnp.zeros((2, rows + 2 * width, columns + 2 * width), jnp.float32)
            else:
                field_ext = with_halo(field, (("grp", 1), ("tile", 2)), width)
            margin = width - 1
            offset = 1 - margin
            span_rows = rows + 2 * margin
            span_cols = columns + 2 * margin
            terms_sub = terms[:, offset : offset + span_rows, offset : offset + span_cols]
            diag_sub = diagonal[:, offset : offset + span_rows, offset : offset + span_cols]
            inside_sub = inside[offset : offset + span_rows, offset : offset + span_cols]
            source_sub = source_ext[:, offset : offset + span_rows, offset : offset + span_cols]
            centre = field_ext[:, 1:-1, 1:-1]
            updated = (
                centre + relax_weight * (source_sub - operate(field_ext, terms_sub)) / diag_sub
            )
            field_ext = jnp.where(inside_sub[None], updated, 0.0)
            field = field_ext
            finished = finished + width
        return field

    source = -(friction_probe[None] * base_velocity)
    increment = relax(source)
    los_got, weight_got = (
        lax.all_to_all(pixel_los, "tile", split_axis=3, concat_axis=1, tiled=True),
        lax.all_to_all(pixel_weight, "tile", split_axis=3, concat_axis=1, tiled=True),
    )
    cell_got, count_got = (
        lax.all_to_all(pixel_cell, "tile", split_axis=3, concat_axis=1, tiled=True),
        lax.all_to_all(pixel_count, "tile", split_axis=3, concat_axis=1, tiled=True),
    )
    slot_cap = cell_got.shape[3]
    live = jnp.arange(slot_cap, dtype=jnp.int32)[None, None, None, :] < count_got
    spot = cell_got.reshape(-1)
    los_x = los_got[:, :, 0].reshape(-1)
    los_y = los_got[:, :, 1].reshape(-1)
    flat = increment.reshape(2, -1)
    predicted = los_x * flat[0][spot] + los_y * flat[1][spot]
    amount = jnp.where(live.reshape(-1), weight_got.reshape(-1) * predicted, 0.0)
    adjoint_source = (
        jnp.zeros((2, rows * columns), jnp.float32)
        .at[:, spot]
        .add(jnp.stack([amount * los_x, amount * los_y]))
        .reshape(2, rows, columns)
    )
    multiplier = relax(adjoint_source)
    hessian_probe = -(base_velocity[0] * multiplier[0] + base_velocity[1] * multiplier[1])
    probe_low = hessian_probe.astype(jnp.bfloat16)
    panel_count = panels.shape[0]
    partial_sum = jnp.dot(
        panels.reshape(panel_count, -1),
        lax.all_gather(probe_low, "grp", axis=0, tiled=True).reshape(-1),
        preferred_element_type=jnp.float32,
    )
    summed = lax.psum(partial_sum, "tile")
    coefficients = lax.all_gather(summed, "grp", axis=0, tiled=True)
    return (increment, hessian_probe, coefficients)


def solution(mesh):
    in_specs = (
        P(None, "grp", "tile"),
        P("grp", "tile"),
        P("grp", "tile"),
        P("grp", "tile"),
        P("grp", "tile", None, None),
        P("grp", "tile", None, None),
        P("grp", "tile", None, None),
        P("grp", "tile", None, None),
        P("grp", None, "tile"),
    )
    out_specs = (P(None, "grp", "tile"), P("grp", "tile"), P())
    return jax.shard_map(
        on_device, mesh=mesh, in_specs=in_specs, out_specs=out_specs, check_vma=False
    )
```

profile of v0, /device:TPU:272, one launch (start us, length us, event | category | flops | bytes accessed | tf_op | source)
XLA Modules:
  0.0 642.7 jit_solution(6764767820685310328)
XLA Ops:
  1.5 5.7 collective-permute-start
  9.2 5.6 collective-permute-done.1
  17.6 5.8 collective-permute-start.3
  29.7 4.8 collective-permute-start.5
  39.3 5.8 collective-permute-start.7
  47.7 3.2 collective-permute-start.8
  50.9 3.6 collective-permute-start.9
  54.5 4.0 collective-permute-done.9
  60.5 5.8 collective-permute-start.11
  68.8 4.2 collective-permute-start.12
  75.6 5.0 collective-permute-done.13
  82.6 5.8 collective-permute-start.15
  91.0 4.8 collective-permute-start.16
  97.7 5.6 collective-permute-done.17
  105.4 5.8 collective-permute-start.19
  116.6 3.9 collective-permute-start.21
  120.5 3.6 collective-permute-done.21
  126.2 5.8 collective-permute-start.23
  134.5 2.8 collective-permute-start.24
  137.3 3.9 collective-permute-start.25
  141.3 3.6 collective-permute-done.25
  146.9 5.8 collective-permute-start.27
  155.3 3.6 collective-permute-start.28
  158.9 3.1 collective-permute-start.29
  162.7 8.0 %all-to-all-start.1 = ((s32[1,1,1,32]{2,1,0,3:T(1,128)}), s32[1,1,1,32]{2,1,0,3:T(1,128)S(1)}, u32[]{:S(2)}, u32[]{:S(2)}) async-start(s32[1,1,1,32]{2,1,0,3:T(1,128)} %copy.44), calls=%async_computation.1 | async-start | bytes 32768 | tf_op jit(solution)/shard_map/all_to_all | solution.py:126
  175.1 11.4 %reduce.3 = f32[2048,2]{1,0:T(8,128)} reduce(f32[2048,1,1,2]{3,2,1,0:T(1,128)} %bitcast.440, f32[]{:T(128)} %broadcast.279), dimensions={1,2}, to_apply=%bitcast.436.reduce_sub_computation | reduce | bytes 32772
  191.1 5.6 collective-permute-start.31
  198.7 7.4 %all-to-all-start = ((s32[1,1,1,2048]{2,1,0,3:T(1,128)}), s32[1,1,1,2048]{2,1,0,3:T(1,128)}, u32[]{:S(2)}, u32[]{:S(2)}) async-start(s32[1,1,1,2048]{2,1,0,3:T(1,128)} %copy.43), calls=%async_computation | async-start | bytes 2097152 | tf_op jit(solution)/shard_map/all_to_all | solution.py:125
  207.7 22.2 %all-to-all-done = s32[1,1,1,2048]{2,1,0,3:T(1,128)} async-done(((s32[1,1,1,2048]{2,1,0,3:T(1,128)}), s32[1,1,1,2048]{2,1,0,3:T(1,128)}, u32[]{:S(2)}, u32[]{:S(2)}) %all-to-all-start) | async-done | bytes 8224 | tf_op jit(solution)/shard_map/all_to_all | solution.py:125
  229.8 9.6 %all-to-all-start.2 = ((f32[1,1,1,2048]{2,1,0,3:T(1,128)}), f32[1,1,1,2048]{2,1,0,3:T(1,128)}, u32[]{:S(2)}, u32[]{:S(2)}) async-start(f32[1,1,1,2048]{2,1,0,3:T(1,128)} %copy.45), calls=%async_computation.2 | async-start | bytes 2097152 | tf_op jit(solution)/shard_map/all_to_all | solution.py:122
  239.5 39.3 %reduce = s32[2048]{0:T(1024)S(1)} reduce(s32[1,1,1,2048]{2,1,0,3:T(1,128)} %all-to-all-done, s32[]{:T(128)} %constant.20.clone.1), dimensions={0,1,2}, to_apply=%all_to_all.14.reduce_sub_computation | reduce | bytes 16388 | tf_op jit(solution)/shard_map/all_to_all | solution.py:125
  278.8 8.3 %all-to-all-start.3 = ((f32[32,1,128]{2,1,0:T(1,128)}), f32[32,1,128]{2,1,0:T(1,128)S(1)}, u32[]{:S(2)}, u32[]{:S(2)}) async-start(f32[32,1,128]{2,1,0:T(1,128)} %reshape.279), calls=%async_computation.3 | async-start | bytes 32768 | tf_op jit(solution)/shard_map/all_to_all | solution.py:121
  287.1 11.8 %gather_fusion = f32[2048]{0:T(1024)S(1)} fusion(f32[8192]{0:T(1024)S(1)} %get-tuple-element.103, s32[2048]{0:T(1024)S(1)} %broadcast_clamp_fusion), kind=kCustom, calls=%fused_computation | custom fusion | bytes 24576 | tf_op jit(solution)/shard_map/gather | solution.py:134
  298.9 11.8 %gather_fusion.1 = f32[2048]{0:T(1024)S(1)} fusion(f32[8192]{0:T(1024)S(1)} %get-tuple-element.104, s32[2048]{0:T(1024)S(1)} %broadcast_clamp_fusion), kind=kCustom, calls=%fused_computation.1 | custom fusion | bytes 24576 | tf_op jit(solution)/shard_map/gather | solution.py:134
  310.7 16.3 %reduce.2 = f32[2048]{0:T(1024)S(1)} reduce(f32[1,1,1,2048]{2,1,0,3:T(1,128)} %all-to-all-done.2, f32[]{:T(128)} %constant.57), dimensions={0,1,2}, to_apply=%all_to_all.16.reduce_sub_computation | reduce | bytes 16388 | tf_op jit(solution)/shard_map/all_to_all | solution.py:122
  333.6 14.0 %scatter_custom_fusion = f32[2,8192]{0,1:T(8,128)} fusion(s32[2048]{0:T(1024)S(1)} %bitcast.453, f32[2048,2]{1,0:T(8,128)} %copy.48, f32[]{:T(128)} %constant.6.clone.1), kind=kCustom, calls=%fused_computation.5 | custom fusion | flops 4096 | bytes 66048 | tf_op jit(solution)/shard_map/scatter-add | solution.py:139
  347.6 2.8 copy.49
  350.5 5.1 collective-permute-start.32
  357.6 5.6 collective-permute-done.33
  365.3 5.8 collective-permute-start.35
  373.6 3.3 collective-permute-start.36
  377.0 3.4 collective-permute-start.37
  380.4 4.5 collective-permute-done.37
  386.9 6.0 collective-permute-start.39
  395.3 4.8 collective-permute-start.40
  402.0 5.6 collective-permute-done.41
  409.7 5.8 collective-permute-start.43
  418.0 2.8 collective-permute-start.44
  420.9 3.9 collective-permute-start.45
  424.8 3.6 collective-permute-done.45
  430.5 5.8 collective-permute-start.47
  441.7 3.9 collective-permute-start.49
  445.6 3.6 collective-permute-done.49
  451.2 5.8 collective-permute-start.51
  459.6 3.3 collective-permute-start.52
  462.9 3.4 collective-permute-start.53
  466.4 4.2 collective-permute-done.53
  472.5 5.8 collective-permute-start.55
  480.9 4.8 collective-permute-start.56
  487.7 5.6 collective-permute-done.57
  495.3 5.8 collective-permute-start.59
  504.4 38.2 %all_gather.6 = bf16[1024,128]{1,0:T(8,128)(2,1)S(1)} all-gather(bf16[64,128]{1,0:T(8,128)(2,1)S(1)} %get-tuple-element.3), channel_id=1, replica_groups=mesh['grp'=16,'tile'=32] {'grp'}, dimensions={0}, use_global_device_ids=true | all-gather | bytes 278528 | tf_op jit(solution)/shard_map/all_gather | solution.py:148
  545.3 53.0 %psum.7 = f32[8]{0:T(128)S(1)} all-reduce(f32[8]{0:T(128)S(1)} %fusion.4), channel_id=1, replica_groups=mesh['grp'=16,'tile'=32] {'tile'}, use_global_device_ids=true, to_apply=%region_1.2 | all-reduce | flops 8 | bytes 64 | tf_op jit(solution)/shard_map/psum | solution.py:151
  598.5 43.7 %all-reduce = f32[128]{0:T(128)} all-reduce(f32[128]{0:T(128)S(1)} %dynamic-update-slice), channel_id=1, replica_groups=mesh['grp'=16,'tile'=32] {'grp'}, use_global_device_ids=true, to_apply=%add | all-reduce | flops 128 | bytes 1024
  (244 shorter events, 112.2 us)
Async XLA Ops:
  1.5 7.7 %collective-permute-start = (f32[2,2,128]{2,1,0:T(2,128)S(1)}, f32[2,2,128]{2,1,0:T(2,128)S(1)}, u32[]{:S(2)}, u32[]{:S(2)}) collective-permute-start(f32[2,2,128]{2,1,0:T(2,128)S(1)} %get-tuple-element.119), channel_id=1, source_target_pairs={{0,32},{32,64},{64,96},{96,128},{128,160},{160,192},{192,224},{224... | collective-permute-start | bytes 6152 | tf_op jit(solution)/shard_map/ppermute | solution.py:20
  7.2 7.6 %collective-permute-start.1 = (f32[2,2,128]{2,1,0:T(2,128)S(1)}, f32[2,2,128]{2,1,0:T(2,128)S(1)}, u32[]{:S(2)}, u32[]{:S(2)}) collective-permute-start(f32[2,2,128]{2,1,0:T(2,128)S(1)} %get-tuple-element.120), channel_id=1, source_target_pairs={{32,0},{64,32},{96,64},{128,96},{160,128},{192,160},{224,192},{256... | collective-permute-start | bytes 6152 | tf_op jit(solution)/shard_map/ppermute | solution.py:22
  15.7 8.4 %collective-permute-start.2 = (f32[2,68,2]{2,1,0:T(8,128)S(1)}, f32[2,68,2]{2,1,0:T(8,128)S(1)}, u32[]{:S(2)}, u32[]{:S(2)}) collective-permute-start(f32[2,68,2]{2,1,0:T(8,128)S(1)} %get-tuple-element.87), channel_id=1, source_target_pairs={{0,1},{1,2},{2,3},{3,4},{4,5},{5,6},{6,7},{7,8},{8,9},{9,10},{10,1... | collective-permute-start | bytes 3272 | tf_op jit(solution)/shard_map/ppermute | solution.py:20
  17.6 7.7 %collective-permute-start.3 = (f32[2,68,2]{2,1,0:T(8,128)S(1)}, f32[2,68,2]{2,1,0:T(8,128)S(1)}, u32[]{:S(2)}, u32[]{:S(2)}) collective-permute-start(f32[2,68,2]{2,1,0:T(8,128)S(1)} %get-tuple-element.88), channel_id=1, source_target_pairs={{1,0},{2,1},{3,2},{4,3},{5,4},{6,5},{7,6},{8,7},{9,8},{10,9},{11,1... | collective-permute-start | bytes 3272 | tf_op jit(solution)/shard_map/ppermute | solution.py:22
  27.8 6.8 %collective-permute-start.4 = (f32[2,1,128]{2,1,0:T(1,128)S(1)}, f32[2,1,128]{2,1,0:T(1,128)S(1)}, u32[]{:S(2)}, u32[]{:S(2)}) collective-permute-start(f32[2,1,128]{2,1,0:T(1,128)S(1)} %get-tuple-element.117), channel_id=1, source_target_pairs={{0,32},{32,64},{64,96},{96,128},{128,160},{160,192},{192,224},{224... | collective-permute-start | bytes 3080 | tf_op jit(solution)/shard_map/ppermute | solution.py:20
  29.7 7.6 %collective-permute-start.5 = (f32[2,1,128]{2,1,0:T(1,128)S(1)}, f32[2,1,128]{2,1,0:T(1,128)S(1)}, u32[]{:S(2)}, u32[]{:S(2)}) collective-permute-start(f32[2,1,128]{2,1,0:T(1,128)S(1)} %get-tuple-element.118), channel_id=1, source_target_pairs={{32,0},{64,32},{96,64},{128,96},{160,128},{192,160},{224,192},{256... | collective-permute-start | bytes 3080 | tf_op jit(solution)/shard_map/ppermute | solution.py:22
  37.4 7.8 %collective-permute-start.6 = (f32[2,66,1]{2,1,0:T(8,128)S(1)}, f32[2,66,1]{2,1,0:T(8,128)S(1)}, u32[]{:S(2)}, u32[]{:S(2)}) collective-permute-start(f32[2,66,1]{2,1,0:T(8,128)S(1)} %get-tuple-element.79), channel_id=1, source_target_pairs={{0,1},{1,2},{2,3},{3,4},{4,5},{5,6},{6,7},{7,8},{8,9},{9,10},{10,1... | collective-permute-start | bytes 1592 | tf_op jit(solution)/shard_map/ppermute | solution.py:20
  39.3 7.7 %collective-permute-start.7 = (f32[2,66,1]{2,1,0:T(8,128)S(1)}, f32[2,66,1]{2,1,0:T(8,128)S(1)}, u32[]{:S(2)}, u32[]{:S(2)}) collective-permute-start(f32[2,66,1]{2,1,0:T(8,128)S(1)} %get-tuple-element.80), channel_id=1, source_target_pairs={{1,0},{2,1},{3,2},{4,3},{5,4},{6,5},{7,6},{8,7},{9,8},{10,9},{11,1... | collective-permute-start | bytes 1592 | tf_op jit(solution)/shard_map/ppermute | solution.py:22
  47.7 6.8 %collective-permute-start.8 = (f32[2,1,128]{2,1,0:T(1,128)S(1)}, f32[2,1,128]{2,1,0:T(1,128)S(1)}, u32[]{:S(2)}, u32[]{:S(2)}) collective-permute-start(f32[2,1,128]{2,1,0:T(1,128)S(1)} %get-tuple-element.115), channel_id=1, source_target_pairs={{0,32},{32,64},{64,96},{96,128},{128,160},{160,192},{192,224},{224... | collective-permute-start | bytes 3080 | tf_op jit(solution)/shard_map/ppermute | solution.py:20
  50.9 7.6 %collective-permute-start.9 = (f32[2,1,128]{2,1,0:T(1,128)S(1)}, f32[2,1,128]{2,1,0:T(1,128)S(1)}, u32[]{:S(2)}, u32[]{:S(2)}) collective-permute-start(f32[2,1,128]{2,1,0:T(1,128)S(1)} %get-tuple-element.116), channel_id=1, source_target_pairs={{32,0},{64,32},{96,64},{128,96},{160,128},{192,160},{224,192},{256... | collective-permute-start | bytes 3080 | tf_op jit(solution)/shard_map/ppermute | solution.py:22
  58.5 7.8 %collective-permute-start.10 = (f32[2,66,1]{2,1,0:T(8,128)S(1)}, f32[2,66,1]{2,1,0:T(8,128)S(1)}, u32[]{:S(2)}, u32[]{:S(2)}) collective-permute-start(f32[2,66,1]{2,1,0:T(8,128)S(1)} %get-tuple-element.77), channel_id=1, source_target_pairs={{0,1},{1,2},{2,3},{3,4},{4,5},{5,6},{6,7},{7,8},{8,9},{9,10},{10,1... | collective-permute-start | bytes 1592 | tf_op jit(solution)/shard_map/ppermute | solution.py:20
  60.5 7.7 %collective-permute-start.11 = (f32[2,66,1]{2,1,0:T(8,128)S(1)}, f32[2,66,1]{2,1,0:T(8,128)S(1)}, u32[]{:S(2)}, u32[]{:S(2)}) collective-permute-start(f32[2,66,1]{2,1,0:T(8,128)S(1)} %get-tuple-element.78), channel_id=1, source_target_pairs={{1,0},{2,1},{3,2},{4,3},{5,4},{6,5},{7,6},{8,7},{9,8},{10,9},{11,1... | collective-permute-start | bytes 1592 | tf_op jit(solution)/shard_map/ppermute | solution.py:22
  68.8 6.8 %collective-permute-start.12 = (f32[2,1,128]{2,1,0:T(1,128)S(1)}, f32[2,1,128]{2,1,0:T(1,128)S(1)}, u32[]{:S(2)}, u32[]{:S(2)}) collective-permute-start(f32[2,1,128]{2,1,0:T(1,128)S(1)} %get-tuple-element.113), channel_id=1, source_target_pairs={{0,32},{32,64},{64,96},{96,128},{128,160},{160,192},{192,224},{224... | collective-permute-start | bytes 3080 | tf_op jit(solution)/shard_map/ppermute | solution.py:20
  73.0 7.6 %collective-permute-start.13 = (f32[2,1,128]{2,1,0:T(1,128)S(1)}, f32[2,1,128]{2,1,0:T(1,128)S(1)}, u32[]{:S(2)}, u32[]{:S(2)}) collective-permute-start(f32[2,1,128]{2,1,0:T(1,128)S(1)} %get-tuple-element.114), channel_id=1, source_target_pairs={{32,0},{64,32},{96,64},{128,96},{160,128},{192,160},{224,192},{256... | collective-permute-start | bytes 3080 | tf_op jit(solution)/shard_map/ppermute | solution.py:22
  80.7 7.8 %collective-permute-start.14 = (f32[2,66,1]{2,1,0:T(8,128)S(1)}, f32[2,66,1]{2,1,0:T(8,128)S(1)}, u32[]{:S(2)}, u32[]{:S(2)}) collective-permute-start(f32[2,66,1]{2,1,0:T(8,128)S(1)} %get-tuple-element.75), channel_id=1, source_target_pairs={{0,1},{1,2},{2,3},{3,4},{4,5},{5,6},{6,7},{7,8},{8,9},{9,10},{10,1... | collective-permute-start | bytes 1592 | tf_op jit(solution)/shard_map/ppermute | solution.py:20
  82.6 7.7 %collective-permute-start.15 = (f32[2,66,1]{2,1,0:T(8,128)S(1)}, f32[2,66,1]{2,1,0:T(8,128)S(1)}, u32[]{:S(2)}, u32[]{:S(2)}) collective-permute-start(f32[2,66,1]{2,1,0:T(8,128)S(1)} %get-tuple-element.76), channel_id=1, source_target_pairs={{1,0},{2,1},{3,2},{4,3},{5,4},{6,5},{7,6},{8,7},{9,8},{10,9},{11,1... | collective-permute-start | bytes 1592 | tf_op jit(solution)/shard_map/ppermute | solution.py:22
  91.0 6.8 %collective-permute-start.16 = (f32[2,1,128]{2,1,0:T(1,128)S(1)}, f32[2,1,128]{2,1,0:T(1,128)S(1)}, u32[]{:S(2)}, u32[]{:S(2)}) collective-permute-start(f32[2,1,128]{2,1,0:T(1,128)S(1)} %get-tuple-element.111), channel_id=1, source_target_pairs={{0,32},{32,64},{64,96},{96,128},{128,160},{160,192},{192,224},{224... | collective-permute-start | bytes 3080 | tf_op jit(solution)/shard_map/ppermute | solution.py:20
  95.8 7.6 %collective-permute-start.17 = (f32[2,1,128]{2,1,0:T(1,128)S(1)}, f32[2,1,128]{2,1,0:T(1,128)S(1)}, u32[]{:S(2)}, u32[]{:S(2)}) collective-permute-start(f32[2,1,128]{2,1,0:T(1,128)S(1)} %get-tuple-element.112), channel_id=1, source_target_pairs={{32,0},{64,32},{96,64},{128,96},{160,128},{192,160},{224,192},{256... | collective-permute-start | bytes 3080 | tf_op jit(solution)/shard_map/ppermute | solution.py:22
  103.5 7.8 %collective-permute-start.18 = (f32[2,66,1]{2,1,0:T(8,128)S(1)}, f32[2,66,1]{2,1,0:T(8,128)S(1)}, u32[]{:S(2)}, u32[]{:S(2)}) collective-permute-start(f32[2,66,1]{2,1,0:T(8,128)S(1)} %get-tuple-element.73), channel_id=1, source_target_pairs={{0,1},{1,2},{2,3},{3,4},{4,5},{5,6},{6,7},{7,8},{8,9},{9,10},{10,1... | collective-permute-start | bytes 1592 | tf_op jit(solution)/shard_map/ppermute | solution.py:20
  105.4 7.7 %collective-permute-start.19 = (f32[2,66,1]{2,1,0:T(8,128)S(1)}, f32[2,66,1]{2,1,0:T(8,128)S(1)}, u32[]{:S(2)}, u32[]{:S(2)}) collective-permute-start(f32[2,66,1]{2,1,0:T(8,128)S(1)} %get-tuple-element.74), channel_id=1, source_target_pairs={{1,0},{2,1},{3,2},{4,3},{5,4},{6,5},{7,6},{8,7},{9,8},{10,9},{11,1... | collective-permute-start | bytes 1592 | tf_op jit(solution)/shard_map/ppermute | solution.py:22
  113.7 6.8 %collective-permute-start.20 = (f32[2,1,128]{2,1,0:T(1,128)S(1)}, f32[2,1,128]{2,1,0:T(1,128)S(1)}, u32[]{:S(2)}, u32[]{:S(2)}) collective-permute-start(f32[2,1,128]{2,1,0:T(1,128)S(1)} %get-tuple-element.109), channel_id=1, source_target_pairs={{0,32},{32,64},{64,96},{96,128},{128,160},{160,192},{192,224},{224... | collective-permute-start | bytes 3080 | tf_op jit(solution)/shard_map/ppermute | solution.py:20
  116.6 7.6 %collective-permute-start.21 = (f32[2,1,128]{2,1,0:T(1,128)S(1)}, f32[2,1,128]{2,1,0:T(1,128)S(1)}, u32[]{:S(2)}, u32[]{:S(2)}) collective-permute-start(f32[2,1,128]{2,1,0:T(1,128)S(1)} %get-tuple-element.110), channel_id=1, source_target_pairs={{32,0},{64,32},{96,64},{128,96},{160,128},{192,160},{224,192},{256... | collective-permute-start | bytes 3080 | tf_op jit(solution)/shard_map/ppermute | solution.py:22
  124.2 7.8 %collective-permute-start.22 = (f32[2,66,1]{2,1,0:T(8,128)S(1)}, f32[2,66,1]{2,1,0:T(8,128)S(1)}, u32[]{:S(2)}, u32[]{:S(2)}) collective-permute-start(f32[2,66,1]{2,1,0:T(8,128)S(1)} %get-tuple-element.71), channel_id=1, source_target_pairs={{0,1},{1,2},{2,3},{3,4},{4,5},{5,6},{6,7},{7,8},{8,9},{9,10},{10,1... | collective-permute-start | bytes 1592 | tf_op jit(solution)/shard_map/ppermute | solution.py:20
  126.2 7.7 %collective-permute-start.23 = (f32[2,66,1]{2,1,0:T(8,128)S(1)}, f32[2,66,1]{2,1,0:T(8,128)S(1)}, u32[]{:S(2)}, u32[]{:S(2)}) collective-permute-start(f32[2,66,1]{2,1,0:T(8,128)S(1)} %get-tuple-element.72), channel_id=1, source_target_pairs={{1,0},{2,1},{3,2},{4,3},{5,4},{6,5},{7,6},{8,7},{9,8},{10,9},{11,1... | collective-permute-start | bytes 1592 | tf_op jit(solution)/shard_map/ppermute | solution.py:22
  134.5 6.8 %collective-permute-start.24 = (f32[2,1,128]{2,1,0:T(1,128)S(1)}, f32[2,1,128]{2,1,0:T(1,128)S(1)}, u32[]{:S(2)}, u32[]{:S(2)}) collective-permute-start(f32[2,1,128]{2,1,0:T(1,128)S(1)} %get-tuple-element.107), channel_id=1, source_target_pairs={{0,32},{32,64},{64,96},{96,128},{128,160},{160,192},{192,224},{224... | collective-permute-start | bytes 3080 | tf_op jit(solution)/shard_map/ppermute | solution.py:20
  137.3 7.6 %collective-permute-start.25 = (f32[2,1,128]{2,1,0:T(1,128)S(1)}, f32[2,1,128]{2,1,0:T(1,128)S(1)}, u32[]{:S(2)}, u32[]{:S(2)}) collective-permute-start(f32[2,1,128]{2,1,0:T(1,128)S(1)} %get-tuple-element.108), channel_id=1, source_target_pairs={{32,0},{64,32},{96,64},{128,96},{160,128},{192,160},{224,192},{256... | collective-permute-start | bytes 3080 | tf_op jit(solution)/shard_map/ppermute | solution.py:22
  145.0 7.8 %collective-permute-start.26 = (f32[2,66,1]{2,1,0:T(8,128)S(1)}, f32[2,66,1]{2,1,0:T(8,128)S(1)}, u32[]{:S(2)}, u32[]{:S(2)}) collective-permute-start(f32[2,66,1]{2,1,0:T(8,128)S(1)} %get-tuple-element.69), channel_id=1, source_target_pairs={{0,1},{1,2},{2,3},{3,4},{4,5},{5,6},{6,7},{7,8},{8,9},{9,10},{10,1... | collective-permute-start | bytes 1592 | tf_op jit(solution)/shard_map/ppermute | solution.py:20
  146.9 7.7 %collective-permute-start.27 = (f32[2,66,1]{2,1,0:T(8,128)S(1)}, f32[2,66,1]{2,1,0:T(8,128)S(1)}, u32[]{:S(2)}, u32[]{:S(2)}) collective-permute-start(f32[2,66,1]{2,1,0:T(8,128)S(1)} %get-tuple-element.70), channel_id=1, source_target_pairs={{1,0},{2,1},{3,2},{4,3},{5,4},{6,5},{7,6},{8,7},{9,8},{10,9},{11,1... | collective-permute-start | bytes 1592 | tf_op jit(solution)/shard_map/ppermute | solution.py:22
  155.3 33.6 %collective-permute-start.28 = (f32[2,1,128]{2,1,0:T(1,128)S(1)}, f32[2,1,128]{2,1,0:T(1,128)S(1)}, u32[]{:S(2)}, u32[]{:S(2)}) collective-permute-start(f32[2,1,128]{2,1,0:T(1,128)S(1)} %get-tuple-element.105), channel_id=1, source_target_pairs={{0,32},{32,64},{64,96},{96,128},{128,160},{160,192},{192,224},{224... | collective-permute-start | bytes 3080 | tf_op jit(solution)/shard_map/ppermute | solution.py:20
  158.9 30.0 %collective-permute-start.29 = (f32[2,1,128]{2,1,0:T(1,128)S(1)}, f32[2,1,128]{2,1,0:T(1,128)S(1)}, u32[]{:S(2)}, u32[]{:S(2)}) collective-permute-start(f32[2,1,128]{2,1,0:T(1,128)S(1)} %get-tuple-element.106), channel_id=1, source_target_pairs={{32,0},{64,32},{96,64},{128,96},{160,128},{192,160},{224,192},{256... | collective-permute-start | bytes 3080 | tf_op jit(solution)/shard_map/ppermute | solution.py:22
  162.7 36.0 %all-to-all-start.1 = ((s32[1,1,1,32]{2,1,0,3:T(1,128)}), s32[1,1,1,32]{2,1,0,3:T(1,128)S(1)}, u32[]{:S(2)}, u32[]{:S(2)}) async-start(s32[1,1,1,32]{2,1,0,3:T(1,128)} %copy.44), calls=%async_computation.1 | async-start | bytes 32768 | tf_op jit(solution)/shard_map/all_to_all | solution.py:126
  189.0 18.0 %collective-permute-start.30 = (f32[2,66,1]{2,1,0:T(8,128)S(1)}, f32[2,66,1]{2,1,0:T(8,128)S(1)}, u32[]{:S(2)}, u32[]{:S(2)}) collective-permute-start(f32[2,66,1]{2,1,0:T(8,128)S(1)} %get-tuple-element.67), channel_id=1, source_target_pairs={{0,1},{1,2},{2,3},{3,4},{4,5},{5,6},{6,7},{7,8},{8,9},{9,10},{10,1... | collective-permute-start | bytes 1592 | tf_op jit(solution)/shard_map/ppermute | solution.py:20
  191.1 15.9 %collective-permute-start.31 = (f32[2,66,1]{2,1,0:T(8,128)S(1)}, f32[2,66,1]{2,1,0:T(8,128)S(1)}, u32[]{:S(2)}, u32[]{:S(2)}) collective-permute-start(f32[2,66,1]{2,1,0:T(8,128)S(1)} %get-tuple-element.68), channel_id=1, source_target_pairs={{1,0},{2,1},{3,2},{4,3},{5,4},{6,5},{7,6},{8,7},{9,8},{10,9},{11,1... | collective-permute-start | bytes 1592 | tf_op jit(solution)/shard_map/ppermute | solution.py:22
  198.7 31.1 %all-to-all-start = ((s32[1,1,1,2048]{2,1,0,3:T(1,128)}), s32[1,1,1,2048]{2,1,0,3:T(1,128)}, u32[]{:S(2)}, u32[]{:S(2)}) async-start(s32[1,1,1,2048]{2,1,0,3:T(1,128)} %copy.43), calls=%async_computation | async-start | bytes 2097152 | tf_op jit(solution)/shard_map/all_to_all | solution.py:125
  229.8 49.0 %all-to-all-start.2 = ((f32[1,1,1,2048]{2,1,0,3:T(1,128)}), f32[1,1,1,2048]{2,1,0,3:T(1,128)}, u32[]{:S(2)}, u32[]{:S(2)}) async-start(f32[1,1,1,2048]{2,1,0,3:T(1,128)} %copy.45), calls=%async_computation.2 | async-start | bytes 2097152 | tf_op jit(solution)/shard_map/all_to_all | solution.py:122
  278.8 48.2 %all-to-all-start.3 = ((f32[32,1,128]{2,1,0:T(1,128)}), f32[32,1,128]{2,1,0:T(1,128)S(1)}, u32[]{:S(2)}, u32[]{:S(2)}) async-start(f32[32,1,128]{2,1,0:T(1,128)} %reshape.279), calls=%async_computation.3 | async-start | bytes 32768 | tf_op jit(solution)/shard_map/all_to_all | solution.py:121
  350.5 7.1 %collective-permute-start.32 = (f32[2,1,128]{2,1,0:T(1,128)S(1)}, f32[2,1,128]{2,1,0:T(1,128)S(1)}, u32[]{:S(2)}, u32[]{:S(2)}) collective-permute-start(f32[2,1,128]{2,1,0:T(1,128)S(1)} %get-tuple-element.101), channel_id=1, source_target_pairs={{0,32},{32,64},{64,96},{96,128},{128,160},{160,192},{192,224},{224... | collective-permute-start | bytes 3080 | tf_op jit(solution)/shard_map/ppermute | solution.py:20
  355.7 7.6 %collective-permute-start.33 = (f32[2,1,128]{2,1,0:T(1,128)S(1)}, f32[2,1,128]{2,1,0:T(1,128)S(1)}, u32[]{:S(2)}, u32[]{:S(2)}) collective-permute-start(f32[2,1,128]{2,1,0:T(1,128)S(1)} %get-tuple-element.102), channel_id=1, source_target_pairs={{32,0},{64,32},{96,64},{128,96},{160,128},{192,160},{224,192},{256... | collective-permute-start | bytes 3080 | tf_op jit(solution)/shard_map/ppermute | solution.py:22
  363.3 7.8 %collective-permute-start.34 = (f32[2,66,1]{2,1,0:T(8,128)S(1)}, f32[2,66,1]{2,1,0:T(8,128)S(1)}, u32[]{:S(2)}, u32[]{:S(2)}) collective-permute-start(f32[2,66,1]{2,1,0:T(8,128)S(1)} %get-tuple-element.65), channel_id=1, source_target_pairs={{0,1},{1,2},{2,3},{3,4},{4,5},{5,6},{6,7},{7,8},{8,9},{9,10},{10,1... | collective-permute-start | bytes 1592 | tf_op jit(solution)/shard_map/ppermute | solution.py:20
  365.3 7.7 %collective-permute-start.35 = (f32[2,66,1]{2,1,0:T(8,128)S(1)}, f32[2,66,1]{2,1,0:T(8,128)S(1)}, u32[]{:S(2)}, u32[]{:S(2)}) collective-permute-start(f32[2,66,1]{2,1,0:T(8,128)S(1)} %get-tuple-element.66), channel_id=1, source_target_pairs={{1,0},{2,1},{3,2},{4,3},{5,4},{6,5},{7,6},{8,7},{9,8},{10,9},{11,1... | collective-permute-start | bytes 1592 | tf_op jit(solution)/shard_map/ppermute | solution.py:22
  373.6 6.8 %collective-permute-start.36 = (f32[2,1,128]{2,1,0:T(1,128)S(1)}, f32[2,1,128]{2,1,0:T(1,128)S(1)}, u32[]{:S(2)}, u32[]{:S(2)}) collective-permute-start(f32[2,1,128]{2,1,0:T(1,128)S(1)} %get-tuple-element.99), channel_id=1, source_target_pairs={{0,32},{32,64},{64,96},{96,128},{128,160},{160,192},{192,224},{224... | collective-permute-start | bytes 3080 | tf_op jit(solution)/shard_map/ppermute | solution.py:20
  377.0 8.0 %collective-permute-start.37 = (f32[2,1,128]{2,1,0:T(1,128)S(1)}, f32[2,1,128]{2,1,0:T(1,128)S(1)}, u32[]{:S(2)}, u32[]{:S(2)}) collective-permute-start(f32[2,1,128]{2,1,0:T(1,128)S(1)} %get-tuple-element.100), channel_id=1, source_target_pairs={{32,0},{64,32},{96,64},{128,96},{160,128},{192,160},{224,192},{256... | collective-permute-start | bytes 3080 | tf_op jit(solution)/shard_map/ppermute | solution.py:22
  385.0 7.9 %collective-permute-start.38 = (f32[2,66,1]{2,1,0:T(8,128)S(1)}, f32[2,66,1]{2,1,0:T(8,128)S(1)}, u32[]{:S(2)}, u32[]{:S(2)}) collective-permute-start(f32[2,66,1]{2,1,0:T(8,128)S(1)} %get-tuple-element.63), channel_id=1, source_target_pairs={{0,1},{1,2},{2,3},{3,4},{4,5},{5,6},{6,7},{7,8},{8,9},{9,10},{10,1... | collective-permute-start | bytes 1592 | tf_op jit(solution)/shard_map/ppermute | solution.py:20
  386.9 7.7 %collective-permute-start.39 = (f32[2,66,1]{2,1,0:T(8,128)S(1)}, f32[2,66,1]{2,1,0:T(8,128)S(1)}, u32[]{:S(2)}, u32[]{:S(2)}) collective-permute-start(f32[2,66,1]{2,1,0:T(8,128)S(1)} %get-tuple-element.64), channel_id=1, source_target_pairs={{1,0},{2,1},{3,2},{4,3},{5,4},{6,5},{7,6},{8,7},{9,8},{10,9},{11,1... | collective-permute-start | bytes 1592 | tf_op jit(solution)/shard_map/ppermute | solution.py:22
  395.3 6.8 %collective-permute-start.40 = (f32[2,1,128]{2,1,0:T(1,128)S(1)}, f32[2,1,128]{2,1,0:T(1,128)S(1)}, u32[]{:S(2)}, u32[]{:S(2)}) collective-permute-start(f32[2,1,128]{2,1,0:T(1,128)S(1)} %get-tuple-element.97), channel_id=1, source_target_pairs={{0,32},{32,64},{64,96},{96,128},{128,160},{160,192},{192,224},{224... | collective-permute-start | bytes 3080 | tf_op jit(solution)/shard_map/ppermute | solution.py:20
  400.1 7.6 %collective-permute-start.41 = (f32[2,1,128]{2,1,0:T(1,128)S(1)}, f32[2,1,128]{2,1,0:T(1,128)S(1)}, u32[]{:S(2)}, u32[]{:S(2)}) collective-permute-start(f32[2,1,128]{2,1,0:T(1,128)S(1)} %get-tuple-element.98), channel_id=1, source_target_pairs={{32,0},{64,32},{96,64},{128,96},{160,128},{192,160},{224,192},{256... | collective-permute-start | bytes 3080 | tf_op jit(solution)/shard_map/ppermute | solution.py:22
  407.8 7.8 %collective-permute-start.42 = (f32[2,66,1]{2,1,0:T(8,128)S(1)}, f32[2,66,1]{2,1,0:T(8,128)S(1)}, u32[]{:S(2)}, u32[]{:S(2)}) collective-permute-start(f32[2,66,1]{2,1,0:T(8,128)S(1)} %get-tuple-element.61), channel_id=1, source_target_pairs={{0,1},{1,2},{2,3},{3,4},{4,5},{5,6},{6,7},{7,8},{8,9},{9,10},{10,1... | collective-permute-start | bytes 1592 | tf_op jit(solution)/shard_map/ppermute | solution.py:20
  409.7 7.7 %collective-permute-start.43 = (f32[2,66,1]{2,1,0:T(8,128)S(1)}, f32[2,66,1]{2,1,0:T(8,128)S(1)}, u32[]{:S(2)}, u32[]{:S(2)}) collective-permute-start(f32[2,66,1]{2,1,0:T(8,128)S(1)} %get-tuple-element.62), channel_id=1, source_target_pairs={{1,0},{2,1},{3,2},{4,3},{5,4},{6,5},{7,6},{8,7},{9,8},{10,9},{11,1... | collective-permute-start | bytes 1592 | tf_op jit(solution)/shard_map/ppermute | solution.py:22
  418.0 6.8 %collective-permute-start.44 = (f32[2,1,128]{2,1,0:T(1,128)S(1)}, f32[2,1,128]{2,1,0:T(1,128)S(1)}, u32[]{:S(2)}, u32[]{:S(2)}) collective-permute-start(f32[2,1,128]{2,1,0:T(1,128)S(1)} %get-tuple-element.95), channel_id=1, source_target_pairs={{0,32},{32,64},{64,96},{96,128},{128,160},{160,192},{192,224},{224... | collective-permute-start | bytes 3080 | tf_op jit(solution)/shard_map/ppermute | solution.py:20
  420.9 7.6 %collective-permute-start.45 = (f32[2,1,128]{2,1,0:T(1,128)S(1)}, f32[2,1,128]{2,1,0:T(1,128)S(1)}, u32[]{:S(2)}, u32[]{:S(2)}) collective-permute-start(f32[2,1,128]{2,1,0:T(1,128)S(1)} %get-tuple-element.96), channel_id=1, source_target_pairs={{32,0},{64,32},{96,64},{128,96},{160,128},{192,160},{224,192},{256... | collective-permute-start | bytes 3080 | tf_op jit(solution)/shard_map/ppermute | solution.py:22
  428.5 7.8 %collective-permute-start.46 = (f32[2,66,1]{2,1,0:T(8,128)S(1)}, f32[2,66,1]{2,1,0:T(8,128)S(1)}, u32[]{:S(2)}, u32[]{:S(2)}) collective-permute-start(f32[2,66,1]{2,1,0:T(8,128)S(1)} %get-tuple-element.59), channel_id=1, source_target_pairs={{0,1},{1,2},{2,3},{3,4},{4,5},{5,6},{6,7},{7,8},{8,9},{9,10},{10,1... | collective-permute-start | bytes 1592 | tf_op jit(solution)/shard_map/ppermute | solution.py:20
  430.5 7.7 %collective-permute-start.47 = (f32[2,66,1]{2,1,0:T(8,128)S(1)}, f32[2,66,1]{2,1,0:T(8,128)S(1)}, u32[]{:S(2)}, u32[]{:S(2)}) collective-permute-start(f32[2,66,1]{2,1,0:T(8,128)S(1)} %get-tuple-element.60), channel_id=1, source_target_pairs={{1,0},{2,1},{3,2},{4,3},{5,4},{6,5},{7,6},{8,7},{9,8},{10,9},{11,1... | collective-permute-start | bytes 1592 | tf_op jit(solution)/shard_map/ppermute | solution.py:22
  438.8 6.8 %collective-permute-start.48 = (f32[2,1,128]{2,1,0:T(1,128)S(1)}, f32[2,1,128]{2,1,0:T(1,128)S(1)}, u32[]{:S(2)}, u32[]{:S(2)}) collective-permute-start(f32[2,1,128]{2,1,0:T(1,128)S(1)} %get-tuple-element.93), channel_id=1, source_target_pairs={{0,32},{32,64},{64,96},{96,128},{128,160},{160,192},{192,224},{224... | collective-permute-start | bytes 3080 | tf_op jit(solution)/shard_map/ppermute | solution.py:20
  441.7 7.6 %collective-permute-start.49 = (f32[2,1,128]{2,1,0:T(1,128)S(1)}, f32[2,1,128]{2,1,0:T(1,128)S(1)}, u32[]{:S(2)}, u32[]{:S(2)}) collective-permute-start(f32[2,1,128]{2,1,0:T(1,128)S(1)} %get-tuple-element.94), channel_id=1, source_target_pairs={{32,0},{64,32},{96,64},{128,96},{160,128},{192,160},{224,192},{256... | collective-permute-start | bytes 3080 | tf_op jit(solution)/shard_map/ppermute | solution.py:22
  449.3 7.8 %collective-permute-start.50 = (f32[2,66,1]{2,1,0:T(8,128)S(1)}, f32[2,66,1]{2,1,0:T(8,128)S(1)}, u32[]{:S(2)}, u32[]{:S(2)}) collective-permute-start(f32[2,66,1]{2,1,0:T(8,128)S(1)} %get-tuple-element.57), channel_id=1, source_target_pairs={{0,1},{1,2},{2,3},{3,4},{4,5},{5,6},{6,7},{7,8},{8,9},{9,10},{10,1... | collective-permute-start | bytes 1592 | tf_op jit(solution)/shard_map/ppermute | solution.py:20
  451.2 7.7 %collective-permute-start.51 = (f32[2,66,1]{2,1,0:T(8,128)S(1)}, f32[2,66,1]{2,1,0:T(8,128)S(1)}, u32[]{:S(2)}, u32[]{:S(2)}) collective-permute-start(f32[2,66,1]{2,1,0:T(8,128)S(1)} %get-tuple-element.58), channel_id=1, source_target_pairs={{1,0},{2,1},{3,2},{4,3},{5,4},{6,5},{7,6},{8,7},{9,8},{10,9},{11,1... | collective-permute-start | bytes 1592 | tf_op jit(solution)/shard_map/ppermute | solution.py:22
  459.6 6.8 %collective-permute-start.52 = (f32[2,1,128]{2,1,0:T(1,128)S(1)}, f32[2,1,128]{2,1,0:T(1,128)S(1)}, u32[]{:S(2)}, u32[]{:S(2)}) collective-permute-start(f32[2,1,128]{2,1,0:T(1,128)S(1)} %get-tuple-element.91), channel_id=1, source_target_pairs={{0,32},{32,64},{64,96},{96,128},{128,160},{160,192},{192,224},{224... | collective-permute-start | bytes 3080 | tf_op jit(solution)/shard_map/ppermute | solution.py:20
  462.9 7.6 %collective-permute-start.53 = (f32[2,1,128]{2,1,0:T(1,128)S(1)}, f32[2,1,128]{2,1,0:T(1,128)S(1)}, u32[]{:S(2)}, u32[]{:S(2)}) collective-permute-start(f32[2,1,128]{2,1,0:T(1,128)S(1)} %get-tuple-element.92), channel_id=1, source_target_pairs={{32,0},{64,32},{96,64},{128,96},{160,128},{192,160},{224,192},{256... | collective-permute-start | bytes 3080 | tf_op jit(solution)/shard_map/ppermute | solution.py:22
  470.6 7.8 %collective-permute-start.54 = (f32[2,66,1]{2,1,0:T(8,128)S(1)}, f32[2,66,1]{2,1,0:T(8,128)S(1)}, u32[]{:S(2)}, u32[]{:S(2)}) collective-permute-start(f32[2,66,1]{2,1,0:T(8,128)S(1)} %get-tuple-element.55), channel_id=1, source_target_pairs={{0,1},{1,2},{2,3},{3,4},{4,5},{5,6},{6,7},{7,8},{8,9},{9,10},{10,1... | collective-permute-start | bytes 1592 | tf_op jit(solution)/shard_map/ppermute | solution.py:20
  472.5 7.7 %collective-permute-start.55 = (f32[2,66,1]{2,1,0:T(8,128)S(1)}, f32[2,66,1]{2,1,0:T(8,128)S(1)}, u32[]{:S(2)}, u32[]{:S(2)}) collective-permute-start(f32[2,66,1]{2,1,0:T(8,128)S(1)} %get-tuple-element.56), channel_id=1, source_target_pairs={{1,0},{2,1},{3,2},{4,3},{5,4},{6,5},{7,6},{8,7},{9,8},{10,9},{11,1... | collective-permute-start | bytes 1592 | tf_op jit(solution)/shard_map/ppermute | solution.py:22
  480.9 6.8 %collective-permute-start.56 = (f32[2,1,128]{2,1,0:T(1,128)S(1)}, f32[2,1,128]{2,1,0:T(1,128)S(1)}, u32[]{:S(2)}, u32[]{:S(2)}) collective-permute-start(f32[2,1,128]{2,1,0:T(1,128)S(1)} %get-tuple-element.89), channel_id=1, source_target_pairs={{0,32},{32,64},{64,96},{96,128},{128,160},{160,192},{192,224},{224... | collective-permute-start | bytes 3080 | tf_op jit(solution)/shard_map/ppermute | solution.py:20
  485.7 7.6 %collective-permute-start.57 = (f32[2,1,128]{2,1,0:T(1,128)S(1)}, f32[2,1,128]{2,1,0:T(1,128)S(1)}, u32[]{:S(2)}, u32[]{:S(2)}) collective-permute-start(f32[2,1,128]{2,1,0:T(1,128)S(1)} %get-tuple-element.90), channel_id=1, source_target_pairs={{32,0},{64,32},{96,64},{128,96},{160,128},{192,160},{224,192},{256... | collective-permute-start | bytes 3080 | tf_op jit(solution)/shard_map/ppermute | solution.py:22
  493.4 9.0 %collective-permute-start.58 = (f32[2,66,1]{2,1,0:T(8,128)S(1)}, f32[2,66,1]{2,1,0:T(8,128)S(1)}, u32[]{:S(2)}, u32[]{:S(2)}) collective-permute-start(f32[2,66,1]{2,1,0:T(8,128)S(1)} %get-tuple-element.53), channel_id=1, source_target_pairs={{0,1},{1,2},{2,3},{3,4},{4,5},{5,6},{6,7},{7,8},{8,9},{9,10},{10,1... | collective-permute-start | bytes 1592 | tf_op jit(solution)/shard_map/ppermute | solution.py:20
  495.3 7.8 %collective-permute-start.59 = (f32[2,66,1]{2,1,0:T(8,128)S(1)}, f32[2,66,1]{2,1,0:T(8,128)S(1)}, u32[]{:S(2)}, u32[]{:S(2)}) collective-permute-start(f32[2,66,1]{2,1,0:T(8,128)S(1)} %get-tuple-element.54), channel_id=1, source_target_pairs={{1,0},{2,1},{3,2},{4,3},{5,4},{6,5},{7,6},{8,7},{9,8},{10,9},{11,1... | collective-permute-start | bytes 1592 | tf_op jit(solution)/shard_map/ppermute | solution.py:22
  (7 other events, 960.5 us)
where the time goes:
time: 655 us; the launch traced here: 643 us
  starting transfers between devices  251 us (38%)
  blocking collectives  135 us (21%)
  waiting for transfers between devices  111 us (17%)
  other arithmetic  95.4 us (15%)
  local copies, waits for them, and re-layouts  44.9 us (7%)
    ppermute x30, starting transfers between devices, with_halo(): lax.ppermute(head, axis, [((i + 1) % count, i) for i in range(ends)])  132 us
    ppermute x30, waiting for transfers between devices, with_halo(): lax.ppermute(head, axis, [((i + 1) % count, i) for i in range(ends)])  87.3 us
    ppermute x30, starting transfers between devices, with_halo(): lax.ppermute(tail, axis, [(i, (i + 1) % count) for i in range(ends)])  85.1 us
    psum x1, blocking collectives, on_device(): summed = lax.psum(partial_sum, 'tile')  53 us
    unnamed x1, blocking collectives  43.7 us
    all_to_all x1, other arithmetic, on_device(): lax.all_to_all(pixel_cell, 'tile', split_axis=3, concat_axis=1, tiled=True)  39.3 us
    all_gather x1, blocking collectives, on_device(): lax.all_gather(probe_low, 'grp', axis=0, tiled=True).reshape(-1)  38.2 us
    gather x2, local copies, waits for them, and re-layouts, on_device(): predicted = los_x * flat[0][spot] + los_y * flat[1][spot]  23.6 us
  transfers between devices with their start and end apart: 64, of which 41 were waited for; matrix products, arithmetic and copies ran while one was open for 16% of the time, Pallas kernels for 0%

commit v1 on v0

v1 whole, which is shorter than its diff:
```python
import functools

import jax
import jax.numpy as jnp
from jax import lax
from jax.experimental import pallas as pl
from jax.experimental.pallas import tpu as pltpu
from jax.sharding import PartitionSpec as P

SWEEPS = 8
RELAX = 0.8
HALO = 8
CAP = 64
LANES = 128
MESH = pl.DeviceIdType.MESH
F32 = jnp.float32
BF16 = jnp.bfloat16


def lane_of(shape):
    return lax.broadcasted_iota(jnp.int32, shape, 1)


def row_of(shape):
    return lax.broadcasted_iota(jnp.int32, shape, 0)


def row_next(a):
    return pltpu.roll(a, a.shape[0] - 1, 0)


def row_prev(a):
    return pltpu.roll(a, 1, 0)


def col_next(a):
    return pltpu.roll(a, a.shape[1] - 1, 1)


def col_prev(a):
    return pltpu.roll(a, 1, 1)


def pack_rims(fields):
    lane = lane_of(fields[0].shape)
    packed = fields[0]
    for index, field in enumerate(fields[1:], 1):
        moved = pltpu.roll(field, 16 * index, 1)
        here = (lane >= 16 * index - 8) & (lane < 16 * index + 8)
        packed = jnp.where(here, moved, packed)
    return packed


def kernel(
    n_grp,
    n_tile,
    base_velocity,
    viscosity,
    friction,
    friction_probe,
    pixel_los,
    pixel_weight,
    pixel_cell,
    pixel_count,
    panels,
    increment_out,
    probe_out,
    coef_out,
    ext,
    pack,
    side_r,
    side_l,
    slots_out,
    slots_in,
    coef,
    src,
    field,
    inc_stage,
    ext2,
    pack2,
    side2_r,
    side2_l,
    probe_stage,
    low_stage,
    column,
    panel_buf,
    part_stage,
    part_in,
    sum_stage,
    sum_in,
    halo_send,
    halo_recv,
    halo2_send,
    halo2_recv,
    local_sem,
    many_send,
    many_recv,
):
    g = lax.axis_index("grp")
    t = lax.axis_index("tile")
    up = lax.rem(g + n_grp - 1, n_grp)
    down = lax.rem(g + 1, n_grp)
    left = lax.rem(t + n_tile - 1, n_tile)
    right = lax.rem(t + 1, n_tile)

    barrier = pltpu.get_barrier_semaphore()

    def greet_tile(k, carry):
        pl.semaphore_signal(barrier, inc=1, device_id=(g, lax.rem(t + k, n_tile)), device_id_type=MESH)
        return carry

    def greet_grp(k, carry):
        pl.semaphore_signal(barrier, inc=1, device_id=(lax.rem(g + k, n_grp), t), device_id_type=MESH)
        return carry

    for a in (up, down):
        for b in (left, right):
            pl.semaphore_signal(barrier, inc=1, device_id=(a, b), device_id_type=MESH)
    lax.fori_loop(1, n_grp, greet_grp, 0)
    lax.fori_loop(1, n_tile, greet_tile, 0)

    panel_copy = pltpu.make_async_copy(panels, panel_buf, local_sem.at[0])
    panel_copy.start()

    bvx = base_velocity[0]
    bvy = base_velocity[1]
    fp = friction_probe[...]
    own = (viscosity[...], friction[...], -(fp * bvx), -(fp * bvy))
    for index in range(4):
        ext[index, HALO : HALO + 64, :] = own[index]
    pack[...] = pack_rims(own)

    odd = lax.rem(t, 2)
    lane1 = lane_of((1, LANES))
    for pair in range(n_tile // 2):
        lanes = slice(pair * LANES, (pair + 1) * LANES)
        count = jnp.where(lane1 < CAP, pixel_count[0, 2 * pair], pixel_count[0, 2 * pair + 1])
        live = lax.rem(lane1, CAP) < count
        block = jnp.concatenate(
            [
                pixel_los[:, lanes],
                jnp.where(live, pixel_weight[:, lanes], 0.0),
                pixel_cell[:, lanes].astype(F32),
            ],
            axis=0,
        )
        slots_out[pair] = jnp.where(odd == 1, pltpu.roll(block, CAP, 1), block)

    pl.semaphore_wait(barrier, n_tile - 1 + n_grp - 1 + 4)

    def rim_copies(block, packed, from_right, from_left, send, recv):
        first, last = pl.ds(HALO, HALO), pl.ds(64, HALO)
        above, middle, below = pl.ds(0, HALO), pl.ds(HALO, 64), pl.ds(64 + HALO, HALO)
        head, tail = pl.ds(0, HALO), pl.ds(64 - HALO, HALO)
        moves = [
            (block.at[:, first], block.at[:, below], (up, t)),
            (block.at[:, last], block.at[:, above], (down, t)),
            (packed, from_right.at[middle], (g, left)),
            (packed, from_left.at[middle], (g, right)),
            (packed.at[head], from_right.at[below], (up, left)),
            (packed.at[head], from_left.at[below], (up, right)),
            (packed.at[tail], from_right.at[above], (down, left)),
            (packed.at[tail], from_left.at[above], (down, right)),
        ]
        return [
            pltpu.make_async_remote_copy(
                src_ref=a,
                dst_ref=b,
                send_sem=send.at[index],
                recv_sem=recv.at[index],
                device_id=target,
                device_id_type=MESH,
            )
            for index, (a, b, target) in enumerate(moves)
        ]

    def wait_bytes(ref, sem):
        pltpu.make_async_copy(ref, ref, sem).wait()

    copies = rim_copies(ext, pack, side_r, side_l, halo_send, halo_recv)
    for copy in copies:
        copy.start()

    def send_list(k, carry):
        owner = lax.rem(t + k, n_tile)
        pltpu.make_async_remote_copy(
            src_ref=slots_out.at[lax.div(owner, 2)],
            dst_ref=slots_in.at[k],
            send_sem=many_send.at[0],
            recv_sem=many_recv.at[0],
            device_id=(g, owner),
            device_id_type=MESH,
        ).start()
        return carry

    lax.fori_loop(1, n_tile, send_list, 0)
    slots_in[0] = slots_out[lax.div(t, 2)]

    for copy in copies:
        copy.wait_recv()

    rows = 64 + 2 * HALO
    lane = lane_of((rows, LANES))
    row = row_of((rows, LANES))

    def widen(block, from_right, from_left):
        merged = jnp.where(lax.rem(lane, 16) < 8, from_right[...], from_left[...])
        fields = []
        for index in range(block.shape[0]):
            beside = merged if index == 0 else pltpu.roll(merged, LANES - 16 * index, 1)
            fields.append(jnp.concatenate([block[index], beside], axis=1))
        return fields

    v, fr, sx, sy = widen(ext, side_r, side_l)
    row_inside = ((row >= HALO) | (g > 0)) & ((row < HALO + 64) | (g < n_grp - 1))
    col_inside = ((lane < HALO) & (t < n_tile - 1)) | ((lane >= LANES - HALO) & (t > 0))
    inside = jnp.concatenate([row_inside, row_inside & col_inside], axis=1)
    v = jnp.where(inside, v, 0.0)
    pair_sum = v + row_next(v)
    east = 0.5 * pair_sum
    west = row_prev(east)
    north = 0.5 * (v + col_next(v))
    south = col_prev(north)
    node_pp = 0.0625 * (pair_sum + col_next(pair_sum))
    node_mp = row_prev(node_pp)
    node_pm = col_prev(node_pp)
    node_mm = col_prev(node_mp)
    diag_x = fr + 2.0 * (east + west) + (north + south)
    diag_y = fr + (east + west) + 2.0 * (north + south)
    inv_x = jnp.where(inside, RELAX / jnp.where(inside, diag_x, 1.0), 0.0)
    inv_y = jnp.where(inside, RELAX / jnp.where(inside, diag_y, 1.0), 0.0)
    for index, term in enumerate((east, west, north, south, node_pp, node_mp, node_pm, node_mm, inv_x, inv_y)):
        coef[index] = term
    src[0] = sx
    src[1] = sy

    def sweep(_, carry):
        cx, cy = field[0], field[1]
        ux, uy = row_next(cx), row_next(cy)
        dx, dy = row_prev(cx), row_prev(cy)
        e, w, n, s = coef[0], coef[1], coef[2], coef[3]
        pp, mp, pm, mm = coef[4], coef[5], coef[6], coef[7]
        ax = 2.0 * (e * ux + w * dx)
        ax += col_next(s * cx + (pm * uy - mm * dy))
        ax += col_prev(n * cx + (mp * dy - pp * uy))
        ay = e * uy + w * dy
        ay += col_next(2.0 * (s * cy) + (pm * ux - mm * dx))
        ay += col_prev(2.0 * (n * cy) + (mp * dx - pp * ux))
        field[0] = (1.0 - RELAX) * cx + coef[8] * (src[0] + ax)
        field[1] = (1.0 - RELAX) * cy + coef[9] * (src[1] + ay)
        return carry

    def relax():
        field[0] = coef[8] * src[0]
        field[1] = coef[9] * src[1]
        lax.fori_loop(1, SWEEPS, sweep, 0)
        return field[0, HALO : HALO + 64, :LANES], field[1, HALO : HALO + 64, :LANES]

    inc_x, inc_y = relax()
    inc_stage[0] = inc_x
    inc_stage[1] = inc_y
    increment_copy = pltpu.make_async_copy(inc_stage, increment_out, local_sem.at[1])
    increment_copy.start()

    wait_bytes(slots_in.at[pl.ds(0, n_tile - 1)], many_recv.at[0])

    def halves(a):
        high = a.astype(BF16)
        return high, (a - high.astype(F32)).astype(BF16)

    xh, xl = halves(inc_x)
    yh, yl = halves(inc_y)
    stacked = jnp.concatenate([xh, yh, xl, yl], axis=0)
    chunk = 2 * LANES
    total = jnp.zeros((256, LANES), F32)
    low_half = lane_of((4, LANES)) < CAP
    for index in range(n_tile * CAP // chunk):
        first = jnp.where(low_half, slots_in[4 * index], slots_in[4 * index + 1])
        second = jnp.where(low_half, slots_in[4 * index + 2], slots_in[4 * index + 3])
        lists = jnp.concatenate([first, second], axis=1)
        los_x, los_y, weight = lists[0:1], lists[1:2], lists[2:3]
        cell = lists[3:4].astype(jnp.int32)
        at_col = row_of((LANES, chunk)) == (cell & (LANES - 1))
        at_row = row_of((64, chunk)) == (cell >> 7)
        col_hot = jnp.where(at_col, 1.0, 0.0).astype(BF16)
        found = jnp.dot(stacked, col_hot, preferred_element_type=F32)
        got_x = jnp.sum(jnp.where(at_row, found[0:64] + found[128:192], 0.0), axis=0, keepdims=True)
        got_y = jnp.sum(jnp.where(at_row, found[64:128] + found[192:256], 0.0), axis=0, keepdims=True)
        amount = weight * (los_x * got_x + los_y * got_y)
        scaled = []
        for value in (amount * los_x, amount * los_y):
            high = value.astype(BF16).astype(F32)
            scaled.append((high, value - high))
        hot = [
            jnp.where(at_row, jnp.broadcast_to(part, (64, chunk)), 0.0)
            for part in (scaled[0][0], scaled[1][0], scaled[0][1], scaled[1][1])
        ]
        hot = jnp.concatenate(hot, axis=0).astype(BF16)
        total += lax.dot_general(hot, col_hot, (((1,), (1,)), ((), ())), preferred_element_type=F32)
    adjoint = (total[0:64] + total[128:192], total[64:128] + total[192:256])

    for index in range(2):
        ext2[index, HALO : HALO + 64, :] = adjoint[index]
    pack2[...] = pack_rims(adjoint)
    copies2 = rim_copies(ext2, pack2, side2_r, side2_l, halo2_send, halo2_recv)
    for copy in copies2:
        copy.start()
    for copy in copies2:
        copy.wait_recv()
    sx2, sy2 = widen(ext2, side2_r, side2_l)
    src[0] = sx2
    src[1] = sy2
    mult_x, mult_y = relax()

    probe = -(base_velocity[0] * mult_x + base_velocity[1] * mult_y)
    probe_low = probe.astype(BF16)
    low_stage[...] = probe_low
    column[g] = probe_low

    def send_probe(k, carry):
        peer = lax.rem(g + k, n_grp)
        pltpu.make_async_remote_copy(
            src_ref=low_stage,
            dst_ref=column.at[g],
            send_sem=many_send.at[1],
            recv_sem=many_recv.at[1],
            device_id=(peer, t),
            device_id_type=MESH,
        ).start()
        return carry

    lax.fori_loop(1, n_grp, send_probe, 0)
    probe_stage[...] = probe
    probe_copy = pltpu.make_async_copy(probe_stage, probe_out, local_sem.at[2])
    probe_copy.start()
    panel_copy.wait()
    wait_bytes(column.at[pl.ds(0, n_grp - 1)], many_recv.at[1])

    def project(block, sums):
        values = column[block].astype(F32)
        start = pl.multiple_of(block * 64, 64)
        return tuple(
            total + jnp.sum((panel_buf[k, pl.ds(start, 64), :].astype(F32) * values).reshape(8, 8, LANES), axis=0)
            for k, total in enumerate(sums)
        )

    sums = lax.fori_loop(0, n_grp, project, tuple(jnp.zeros((8, LANES), F32) for _ in range(8)))
    partial = jnp.concatenate([jnp.sum(s, axis=0, keepdims=True) for s in sums], axis=0)
    part_stage[...] = partial
    part_in[t] = partial

    def send_part(k, carry):
        peer = lax.rem(t + k, n_tile)
        pltpu.make_async_remote_copy(
            src_ref=part_stage,
            dst_ref=part_in.at[t],
            send_sem=many_send.at[2],
            recv_sem=many_recv.at[2],
            device_id=(g, peer),
            device_id_type=MESH,
        ).start()
        return carry

    lax.fori_loop(1, n_tile, send_part, 0)
    wait_bytes(part_in.at[pl.ds(0, n_tile - 1)], many_recv.at[2])
    summed = jnp.sum(jnp.sum(part_in[...], axis=0), axis=1, keepdims=True)
    mine = lane_of((8, LANES)) == 8 * g + row_of((8, LANES))
    placed = jnp.where(mine, jnp.broadcast_to(summed, (8, LANES)), 0.0)
    sum_stage[...] = placed
    sum_in[g] = placed

    def send_sum(k, carry):
        peer = lax.rem(g + k, n_grp)
        pltpu.make_async_remote_copy(
            src_ref=sum_stage,
            dst_ref=sum_in.at[g],
            send_sem=many_send.at[3],
            recv_sem=many_recv.at[3],
            device_id=(peer, t),
            device_id_type=MESH,
        ).start()
        return carry

    lax.fori_loop(1, n_grp, send_sum, 0)
    wait_bytes(sum_in.at[pl.ds(0, n_grp - 1)], many_recv.at[3])
    coef_out[...] = jnp.sum(jnp.sum(sum_in[...], axis=0), axis=0, keepdims=True)

    for copy in copies + copies2:
        copy.wait_send()
    wait_bytes(slots_in.at[pl.ds(0, n_tile - 1)], many_send.at[0])
    wait_bytes(column.at[pl.ds(0, n_grp - 1)], many_send.at[1])
    wait_bytes(part_in.at[pl.ds(0, n_tile - 1)], many_send.at[2])
    wait_bytes(sum_in.at[pl.ds(0, n_grp - 1)], many_send.at[3])
    increment_copy.wait()
    probe_copy.wait()


def on_device(n_grp, n_tile, base_velocity, viscosity, friction, friction_probe, pixel_los, pixel_weight, pixel_cell, pixel_count, panels):
    slots = pixel_los.shape[-1]
    panel_rows = panels.shape[1]
    vmem = pl.BlockSpec(memory_space=pltpu.VMEM)
    anywhere = pl.BlockSpec(memory_space=pl.ANY)
    wide = 64 + 2 * HALO
    increment, probe, coefficients = pl.pallas_call(
        functools.partial(kernel, n_grp, n_tile),
        out_shape=(
            jax.ShapeDtypeStruct((2, 64, LANES), F32),
            jax.ShapeDtypeStruct((64, LANES), F32),
            jax.ShapeDtypeStruct((1, LANES), F32),
        ),
        in_specs=[vmem] * 7 + [pl.BlockSpec(memory_space=pltpu.SMEM), anywhere],
        out_specs=(anywhere, anywhere, vmem),
        scratch_shapes=[
            pltpu.VMEM((4, wide, LANES), F32),
            pltpu.VMEM((64, LANES), F32),
            pltpu.VMEM((wide, LANES), F32),
            pltpu.VMEM((wide, LANES), F32),
            pltpu.VMEM((n_tile // 2, 4, LANES), F32),
            pltpu.VMEM((n_tile, 4, LANES), F32),
            pltpu.VMEM((10, wide, 2 * LANES), F32),
            pltpu.VMEM((2, wide, 2 * LANES), F32),
            pltpu.VMEM((2, wide, 2 * LANES), F32),
            pltpu.VMEM((2, 64, LANES), F32),
            pltpu.VMEM((2, wide, LANES), F32),
            pltpu.VMEM((64, LANES), F32),
            pltpu.VMEM((wide, LANES), F32),
            pltpu.VMEM((wide, LANES), F32),
            pltpu.VMEM((64, LANES), F32),
            pltpu.VMEM((64, LANES), BF16),
            pltpu.VMEM((n_grp, 64, LANES), BF16),
            pltpu.VMEM((8, panel_rows, LANES), BF16),
            pltpu.VMEM((8, LANES), F32),
            pltpu.VMEM((n_tile, 8, LANES), F32),
            pltpu.VMEM((8, LANES), F32),
            pltpu.VMEM((n_grp, 8, LANES), F32),
            pltpu.SemaphoreType.DMA((8,)),
            pltpu.SemaphoreType.DMA((8,)),
            pltpu.SemaphoreType.DMA((8,)),
            pltpu.SemaphoreType.DMA((8,)),
            pltpu.SemaphoreType.DMA((3,)),
            pltpu.SemaphoreType.DMA((4,)),
            pltpu.SemaphoreType.DMA((4,)),
        ],
        compiler_params=pltpu.CompilerParams(
            collective_id=0, has_side_effects=True, vmem_limit_bytes=24 * 1024 * 1024
        ),
    )(
        base_velocity,
        viscosity,
        friction,
        friction_probe,
        pixel_los.reshape(2, slots),
        pixel_weight.reshape(1, slots),
        pixel_cell.reshape(1, slots),
        pixel_count.reshape(1, n_tile),
        panels,
    )
    return increment, probe, coefficients.reshape(LANES)[: 8 * n_grp]


def solution(mesh):
    in_specs = (
        P(None, "grp", "tile"),
        P("grp", "tile"),
        P("grp", "tile"),
        P("grp", "tile"),
        P("grp", "tile", None, None),
        P("grp", "tile", None, None),
        P("grp", "tile", None, None),
        P("grp", "tile", None, None),
        P("grp", None, "tile"),
    )
    out_specs = (P(None, "grp", "tile"), P("grp", "tile"), P())
    body = functools.partial(on_device, mesh.shape["grp"], mesh.shape["tile"])
    return jax.shard_map(body, mesh=mesh, in_specs=in_specs, out_specs=out_specs, check_vma=False)
```

time: 655 us -> 64.6 us (0.10)
  the two profiles are of different devices: /device:TPU:272 before, /device:TPU:1 now
where the time goes in v1:
time: 64.6 us; the launch traced here: 64 us
  Pallas kernels  54.1 us (84%)
  local copies, waits for them, and re-layouts  9.22 us (14%)
  between operations  0.66 us (1%)
    pallas_call x1, Pallas kernels, on_device(): pl.pallas_call(functools.partial(kernel, n_grp, n_tile), out_shape=(jax.S...  54.1 us
    unnamed x21, local copies, waits for them, and re-layouts  9.22 us

profile of v1, /device:TPU:1, one launch (start us, length us, event | category | flops | bytes accessed | tf_op | source)
XLA Modules:
  0.0 64.0 jit_solution(6959245853562591718)
XLA Ops:
  0.6 0.0 copy-start
  0.6 1.6 %copy-done = bf16[8,1024,128]{2,1,0:T(8,128)(2,1)S(1)} copy-done((bf16[8,1024,128]{2,1,0:T(8,128)(2,1)S(1)}, bf16[8,1024,128]{2,1,0:T(8,128)(2,1)}, u32[]{:S(2)}) %copy-start) | copy-done | bytes 2097176
  2.2 0.0 copy-start.1
  2.2 0.8 %copy-done.1 = f32[2,64,128]{2,1,0:T(8,128)S(1)} copy-done((f32[2,64,128]{2,1,0:T(8,128)S(1)}, f32[2,64,128]{2,1,0:T(8,128)}, u32[]{:S(2)}) %copy-start.1) | copy-done | bytes 65560
  3.1 0.0 copy-start.2
  3.1 0.8 %copy-done.2 = f32[64,128]{1,0:T(8,128)S(1)} copy-done((f32[64,128]{1,0:T(8,128)S(1)}, f32[64,128]{1,0:T(8,128)}, u32[]{:S(2)}) %copy-start.2) | copy-done | bytes 32792
  3.8 0.0 copy-start.3
  3.8 0.8 %copy-done.3 = f32[64,128]{1,0:T(8,128)S(1)} copy-done((f32[64,128]{1,0:T(8,128)S(1)}, f32[64,128]{1,0:T(8,128)}, u32[]{:S(2)}) %copy-start.3) | copy-done | bytes 32792
  4.6 0.0 copy-start.4
  4.6 0.8 %copy-done.4 = f32[64,128]{1,0:T(8,128)S(1)} copy-done((f32[64,128]{1,0:T(8,128)S(1)}, f32[64,128]{1,0:T(8,128)}, u32[]{:S(2)}) %copy-start.4) | copy-done | bytes 32792
  5.3 0.0 copy-start.5
  5.3 0.7 %copy-done.5 = f32[1,1,2,2048]{3,2,1,0:T(2,128)S(1)} copy-done((f32[1,1,2,2048]{3,2,1,0:T(2,128)S(1)}, f32[1,1,2,2048]{3,2,1,0:T(2,128)}, u32[]{:S(2)}) %copy-start.5) | copy-done | bytes 16408
  6.1 0.0 copy-start.6
  6.1 0.7 %copy-done.6 = f32[1,1,1,2048]{3,2,1,0:T(1,128)S(1)} copy-done((f32[1,1,1,2048]{3,2,1,0:T(1,128)S(1)}, f32[1,1,1,2048]{3,2,1,0:T(1,128)}, u32[]{:S(2)}) %copy-start.6) | copy-done | bytes 8216
  6.8 0.0 copy-start.7
  6.8 0.7 %copy-done.7 = s32[1,1,1,2048]{3,2,1,0:T(1,128)S(1)} copy-done((s32[1,1,1,2048]{3,2,1,0:T(1,128)S(1)}, s32[1,1,1,2048]{3,2,1,0:T(1,128)}, u32[]{:S(2)}) %copy-start.7) | copy-done | bytes 8216
  7.5 0.0 copy-start.8
  7.5 0.7 %copy-done.8 = s32[1,1,1,32]{3,2,1,0:T(1,128)S(1)} copy-done((s32[1,1,1,32]{3,2,1,0:T(1,128)S(1)}, s32[1,1,1,32]{3,2,1,0:T(1,128)}, u32[]{:S(2)}) %copy-start.8) | copy-done | bytes 152
  8.1 54.1 %shard_map.112 = (f32[2,64,128]{2,1,0:T(8,128)S(1)}, f32[64,128]{1,0:T(8,128)S(1)}, f32[1,128]{1,0:T(1,128)S(1)}) custom-call(f32[2,64,128]{2,1,0:T(8,128)S(1)} %copy-done.1, f32[64,128]{1,0:T(8,128)S(1)} %copy-done.2, f32[64,128]{1,0:T(8,128)S(1)} %copy-done.3, f32[64,128]{1,0:T(8,128)S(1)} %copy-done.4, f32[2,2048]{1,0:T(2,128)S(1)} %bitcast.5, ...), custom_call_target="tpu_custom_call" | custom-call | tf_op jit(solution)/shard_map/pallas_call | solution.py:404
  62.3 0.6 copy.15
  62.9 0.6 copy.16
  63.5 0.5 copy.17
Async XLA Ops:
  0.6 1.6 %copy-start = (bf16[8,1024,128]{2,1,0:T(8,128)(2,1)S(1)}, bf16[8,1024,128]{2,1,0:T(8,128)(2,1)}, u32[]{:S(2)}) copy-start(bf16[8,1024,128]{2,1,0:T(8,128)(2,1)} %panels.1) | copy-start | bytes 6291460
  2.2 0.8 %copy-start.1 = (f32[2,64,128]{2,1,0:T(8,128)S(1)}, f32[2,64,128]{2,1,0:T(8,128)}, u32[]{:S(2)}) copy-start(f32[2,64,128]{2,1,0:T(8,128)} %base_velocity.1) | copy-start | bytes 196612
  3.1 0.8 %copy-start.2 = (f32[64,128]{1,0:T(8,128)S(1)}, f32[64,128]{1,0:T(8,128)}, u32[]{:S(2)}) copy-start(f32[64,128]{1,0:T(8,128)} %viscosity.1) | copy-start | bytes 98308
  3.8 0.8 %copy-start.3 = (f32[64,128]{1,0:T(8,128)S(1)}, f32[64,128]{1,0:T(8,128)}, u32[]{:S(2)}) copy-start(f32[64,128]{1,0:T(8,128)} %friction.1) | copy-start | bytes 98308
  4.6 0.8 %copy-start.4 = (f32[64,128]{1,0:T(8,128)S(1)}, f32[64,128]{1,0:T(8,128)}, u32[]{:S(2)}) copy-start(f32[64,128]{1,0:T(8,128)} %friction_probe.1) | copy-start | bytes 98308
  5.3 0.7 %copy-start.5 = (f32[1,1,2,2048]{3,2,1,0:T(2,128)S(1)}, f32[1,1,2,2048]{3,2,1,0:T(2,128)}, u32[]{:S(2)}) copy-start(f32[1,1,2,2048]{3,2,1,0:T(2,128)} %param.13) | copy-start | bytes 49156
  6.1 0.7 %copy-start.6 = (f32[1,1,1,2048]{3,2,1,0:T(1,128)S(1)}, f32[1,1,1,2048]{3,2,1,0:T(1,128)}, u32[]{:S(2)}) copy-start(f32[1,1,1,2048]{3,2,1,0:T(1,128)} %param.14) | copy-start | bytes 24580
  6.8 0.7 %copy-start.7 = (s32[1,1,1,2048]{3,2,1,0:T(1,128)S(1)}, s32[1,1,1,2048]{3,2,1,0:T(1,128)}, u32[]{:S(2)}) copy-start(s32[1,1,1,2048]{3,2,1,0:T(1,128)} %param.15) | copy-start | bytes 24580
  7.5 0.7 %copy-start.8 = (s32[1,1,1,32]{3,2,1,0:T(1,128)S(1)}, s32[1,1,1,32]{3,2,1,0:T(1,128)}, u32[]{:S(2)}) copy-start(s32[1,1,1,32]{3,2,1,0:T(1,128)} %param.16) | copy-start | bytes 388

commit v2 on v1

--- a/solution.py
+++ b/solution.py
@@ -43,17 +43,51 @@
 
 def pack_rims(fields):
     lane = lane_of(fields[0].shape)
-    packed = fields[0]
+    packed = pltpu.roll(fields[0], 8, 1)
     for index, field in enumerate(fields[1:], 1):
-        moved = pltpu.roll(field, 16 * index, 1)
-        here = (lane >= 16 * index - 8) & (lane < 16 * index + 8)
-        packed = jnp.where(here, moved, packed)
+        moved = pltpu.roll(field, 16 * index + 8, 1)
+        packed = jnp.where(lane >= 16 * index, moved, packed)
     return packed
+
+
+def fold_rows(packed, width):
+    high = width // 2
+    folded = packed[0:high]
+    lane = lane_of(folded.shape)
+    for index in range(1, LANES // width):
+        moved = pltpu.roll(packed[index * high : (index + 1) * high], index * width, 1)
+        folded = jnp.where(lane >= index * width, moved, folded)
+    return folded
+
+
+def unfold_rows(folded, width):
+    parts = [folded] + [pltpu.roll(folded, LANES - index * width, 1) for index in range(1, LANES // width)]
+    return jnp.concatenate(parts, axis=0)
+
+
+def ring(offset, size):
+    return min(offset % size, -offset % size)
+
+
+def far_first(pairs, distance):
+    return sorted((p for p in pairs if any(p)), key=lambda p: (-distance(*p), p))
 
 
 def kernel(
     n_grp,
     n_tile,
+    base_velocity_in,
+    viscosity_in,
+    friction_in,
+    friction_probe_in,
+    pixel_los_in,
+    pixel_weight_in,
+    pixel_cell_in,
+    pixel_count_in,
+    panels,
+    increment_out,
+    probe_out,
+    coef_out,
     base_velocity,
     viscosity,
     friction,
@@ -62,10 +96,6 @@
     pixel_weight,
     pixel_cell,
     pixel_count,
-    panels,
-    increment_out,
-    probe_out,
-    coef_out,
     ext,
     pack,
     side_r,
@@ -84,9 +114,7 @@
     low_stage,
     column,
     panel_buf,
-    part_stage,
     part_in,
-    sum_stage,
     sum_in,
     halo_send,
     halo_recv,
@@ -103,33 +131,86 @@
     left = lax.rem(t + n_tile - 1, n_tile)
     right = lax.rem(t + 1, n_tile)
 
+    y_size = 4
+    x_size = n_grp // y_size
+    z_size = n_tile // 4
+    x, y_hi = lax.div(g, y_size), lax.rem(g, y_size)
+    z, y_lo, core = lax.div(t, 4), lax.rem(lax.div(t, 2), 2), lax.rem(t, 2)
+    y = 2 * y_hi + y_lo
+
+    def tile_peer(dz, flip):
+        lo = 1 - y_lo if flip >= 2 else y_lo
+        side = 1 - core if flip % 2 else core
+        return (g, 4 * lax.rem(z + dz, z_size) + 2 * lo + side)
+
+    def grp_peer(dx, dy):
+        return (y_size * lax.rem(x + dx, x_size) + lax.rem(y_hi + dy, y_size), t)
+
+    def plane_peer(dx, dy):
+        there = lax.rem(y + dy, 2 * y_size)
+        return (y_size * lax.rem(x + dx, x_size) + lax.div(there, 2), 4 * z + 2 * lax.rem(there, 2) + core)
+
+    def line_peer(dz, flip):
+        return (g, 4 * lax.rem(z + dz, z_size) + 2 * y_lo + (1 - core if flip else core))
+
+    tile_offsets = far_first(
+        [(dz, flip) for dz in range(z_size) for flip in range(4)], lambda dz, flip: ring(dz, z_size) + (flip >= 2)
+    )
+    grp_offsets = far_first(
+        [(dx, dy) for dx in range(x_size) for dy in range(y_size)],
+        lambda dx, dy: ring(dx, x_size) + 2 * ring(dy, y_size),
+    )
+    plane_offsets = far_first(
+        [(dx, dy) for dx in range(x_size) for dy in range(2 * y_size)],
+        lambda dx, dy: ring(dx, x_size) + ring(dy, 2 * y_size),
+    )
+    line_offsets = far_first(
+        [(dz, flip) for dz in range(z_size) for flip in range(2)], lambda dz, flip: ring(dz, z_size)
+    )
+
     barrier = pltpu.get_barrier_semaphore()
-
-    def greet_tile(k, carry):
-        pl.semaphore_signal(barrier, inc=1, device_id=(g, lax.rem(t + k, n_tile)), device_id_type=MESH)
-        return carry
-
-    def greet_grp(k, carry):
-        pl.semaphore_signal(barrier, inc=1, device_id=(lax.rem(g + k, n_grp), t), device_id_type=MESH)
-        return carry
-
-    for a in (up, down):
-        for b in (left, right):
-            pl.semaphore_signal(barrier, inc=1, device_id=(a, b), device_id_type=MESH)
-    lax.fori_loop(1, n_grp, greet_grp, 0)
-    lax.fori_loop(1, n_tile, greet_tile, 0)
+    corners = [(a, b) for a in (up, down) for b in (left, right)]
+    across = [plane_peer(*p) for p in plane_offsets if p[1] % 2]
+    peers = [grp_peer(*p) for p in grp_offsets] + corners + across + [tile_peer(*p) for p in tile_offsets if p != (0, 2)]
+    for peer in peers:
+        pl.semaphore_signal(barrier, inc=1, device_id=peer, device_id_type=MESH)
+
+    loads = [
+        pltpu.make_async_copy(a, b, local_sem.at[3 + index])
+        for index, (a, b) in enumerate(
+            [
+                (base_velocity_in, base_velocity),
+                (viscosity_in, viscosity),
+                (friction_in, friction),
+                (friction_probe_in, friction_probe),
+                (pixel_los_in.at[0, 0], pixel_los),
+                (pixel_weight_in.at[0, 0], pixel_weight),
+                (pixel_cell_in.at[0, 0], pixel_cell),
+                (pixel_count_in.at[0, 0], pixel_count),
+            ]
+        )
+    ]
+    for load in loads:
+        load.start()
 
     panel_copy = pltpu.make_async_copy(panels, panel_buf, local_sem.at[0])
     panel_copy.start()
 
+    for load in loads[:4]:
+        load.wait()
     bvx = base_velocity[0]
     bvy = base_velocity[1]
     fp = friction_probe[...]
     own = (viscosity[...], friction[...], -(fp * bvx), -(fp * bvy))
     for index in range(4):
         ext[index, HALO : HALO + 64, :] = own[index]
-    pack[...] = pack_rims(own)
-
+    packed = pack_rims(own)
+    pack[0:8] = packed[0:8]
+    pack[8:40] = fold_rows(packed, 64)
+    pack[40:48] = packed[56:64]
+
+    for load in loads[4:]:
+        load.wait()
     odd = lax.rem(t, 2)
     lane1 = lane_of((1, LANES))
     for pair in range(n_tile // 2):
@@ -146,21 +227,22 @@
         )
         slots_out[pair] = jnp.where(odd == 1, pltpu.roll(block, CAP, 1), block)
 
-    pl.semaphore_wait(barrier, n_tile - 1 + n_grp - 1 + 4)
+    pl.semaphore_wait(barrier, len(peers))
 
     def rim_copies(block, packed, from_right, from_left, send, recv):
         first, last = pl.ds(HALO, HALO), pl.ds(64, HALO)
-        above, middle, below = pl.ds(0, HALO), pl.ds(HALO, 64), pl.ds(64 + HALO, HALO)
-        head, tail = pl.ds(0, HALO), pl.ds(64 - HALO, HALO)
+        above, below = pl.ds(0, HALO), pl.ds(64 + HALO, HALO)
+        high = packed.shape[0] - 16
+        head, middle, tail = pl.ds(0, 8), pl.ds(8, high), pl.ds(8 + high, 8)
         moves = [
+            (packed.at[head], from_right.at[tail], (up, left)),
+            (packed.at[head], from_left.at[tail], (up, right)),
+            (packed.at[tail], from_right.at[head], (down, left)),
+            (packed.at[tail], from_left.at[head], (down, right)),
             (block.at[:, first], block.at[:, below], (up, t)),
             (block.at[:, last], block.at[:, above], (down, t)),
-            (packed, from_right.at[middle], (g, left)),
-            (packed, from_left.at[middle], (g, right)),
-            (packed.at[head], from_right.at[below], (up, left)),
-            (packed.at[head], from_left.at[below], (up, right)),
-            (packed.at[tail], from_right.at[above], (down, left)),
-            (packed.at[tail], from_left.at[above], (down, right)),
+            (packed.at[middle], from_right.at[middle], (g, left)),
+            (packed.at[middle], from_left.at[middle], (g, right)),
         ]
         return [
             pltpu.make_async_remote_copy(
@@ -181,19 +263,16 @@
     for copy in copies:
         copy.start()
 
-    def send_list(k, carry):
-        owner = lax.rem(t + k, n_tile)
+    for dz, flip in tile_offsets:
+        peer = tile_peer(dz, flip)
         pltpu.make_async_remote_copy(
-            src_ref=slots_out.at[lax.div(owner, 2)],
-            dst_ref=slots_in.at[k],
+            src_ref=slots_out.at[lax.div(peer[1], 2)],
+            dst_ref=slots_in.at[4 * dz + flip],
             send_sem=many_send.at[0],
             recv_sem=many_recv.at[0],
-            device_id=(g, owner),
+            device_id=peer,
             device_id_type=MESH,
         ).start()
-        return carry
-
-    lax.fori_loop(1, n_tile, send_list, 0)
     slots_in[0] = slots_out[lax.div(t, 2)]
 
     for copy in copies:
@@ -204,10 +283,13 @@
     row = row_of((rows, LANES))
 
     def widen(block, from_right, from_left):
-        merged = jnp.where(lax.rem(lane, 16) < 8, from_right[...], from_left[...])
+        merged = jnp.where(lax.rem(lane_of(from_right.shape), 16) >= 8, from_right[...], from_left[...])
+        high = merged.shape[0] - 16
+        middle = unfold_rows(merged[8 : 8 + high], 2 * high)
+        merged = jnp.concatenate([merged[0:8], middle, merged[8 + high :]], axis=0)
         fields = []
         for index in range(block.shape[0]):
-            beside = merged if index == 0 else pltpu.roll(merged, LANES - 16 * index, 1)
+            beside = pltpu.roll(merged, LANES - 16 * index - 8, 1)
             fields.append(jnp.concatenate([block[index], beside], axis=1))
         return fields
 
@@ -301,7 +383,10 @@
 
     for index in range(2):
         ext2[index, HALO : HALO + 64, :] = adjoint[index]
-    pack2[...] = pack_rims(adjoint)
+    packed2 = pack_rims(adjoint)
+    pack2[0:8] = packed2[0:8]
+    pack2[8:24] = fold_rows(packed2, 32)
+    pack2[24:32] = packed2[56:64]
     copies2 = rim_copies(ext2, pack2, side2_r, side2_l, halo2_send, halo2_recv)
     for copy in copies2:
         copy.start()
@@ -317,19 +402,15 @@
     low_stage[...] = probe_low
     column[g] = probe_low
 
-    def send_probe(k, carry):
-        peer = lax.rem(g + k, n_grp)
+    for offset in grp_offsets:
         pltpu.make_async_remote_copy(
             src_ref=low_stage,
             dst_ref=column.at[g],
             send_sem=many_send.at[1],
             recv_sem=many_recv.at[1],
-            device_id=(peer, t),
+            device_id=grp_peer(*offset),
             device_id_type=MESH,
         ).start()
-        return carry
-
-    lax.fori_loop(1, n_grp, send_probe, 0)
     probe_stage[...] = probe
     probe_copy = pltpu.make_async_copy(probe_stage, probe_out, local_sem.at[2])
     probe_copy.start()
@@ -346,51 +427,33 @@
 
     sums = lax.fori_loop(0, n_grp, project, tuple(jnp.zeros((8, LANES), F32) for _ in range(8)))
     partial = jnp.concatenate([jnp.sum(s, axis=0, keepdims=True) for s in sums], axis=0)
-    part_stage[...] = partial
-    part_in[t] = partial
-
-    def send_part(k, carry):
-        peer = lax.rem(t + k, n_tile)
-        pltpu.make_async_remote_copy(
-            src_ref=part_stage,
-            dst_ref=part_in.at[t],
-            send_sem=many_send.at[2],
-            recv_sem=many_recv.at[2],
-            device_id=(g, peer),
-            device_id_type=MESH,
-        ).start()
-        return carry
-
-    lax.fori_loop(1, n_tile, send_part, 0)
-    wait_bytes(part_in.at[pl.ds(0, n_tile - 1)], many_recv.at[2])
-    summed = jnp.sum(jnp.sum(part_in[...], axis=0), axis=1, keepdims=True)
+    partial = jnp.sum(partial, axis=1, keepdims=True)
     mine = lane_of((8, LANES)) == 8 * g + row_of((8, LANES))
-    placed = jnp.where(mine, jnp.broadcast_to(summed, (8, LANES)), 0.0)
-    sum_stage[...] = placed
-    sum_in[g] = placed
-
-    def send_sum(k, carry):
-        peer = lax.rem(g + k, n_grp)
-        pltpu.make_async_remote_copy(
-            src_ref=sum_stage,
-            dst_ref=sum_in.at[g],
-            send_sem=many_send.at[3],
-            recv_sem=many_recv.at[3],
-            device_id=(peer, t),
-            device_id_type=MESH,
-        ).start()
-        return carry
-
-    lax.fori_loop(1, n_grp, send_sum, 0)
-    wait_bytes(sum_in.at[pl.ds(0, n_grp - 1)], many_recv.at[3])
-    coef_out[...] = jnp.sum(jnp.sum(sum_in[...], axis=0), axis=0, keepdims=True)
+    placed = jnp.sum(jnp.where(mine, jnp.broadcast_to(partial, (8, LANES)), 0.0), axis=0, keepdims=True)
+
+    def sum_over(value, landing, offsets, peer, index):
+        landing[0] = value
+        for slot, offset in enumerate(offsets, 1):
+            pltpu.make_async_remote_copy(
+                src_ref=landing.at[0],
+                dst_ref=landing.at[slot],
+                send_sem=many_send.at[index],
+                recv_sem=many_recv.at[index],
+                device_id=peer(*offset),
+                device_id_type=MESH,
+            ).start()
+        wait_bytes(landing.at[pl.ds(1, len(offsets))], many_recv.at[index])
+        return jnp.sum(landing[...], axis=0)
+
+    plane_sum = sum_over(placed, part_in, plane_offsets, plane_peer, 2)
+    coef_out[...] = sum_over(plane_sum, sum_in, line_offsets, line_peer, 3)
 
     for copy in copies + copies2:
         copy.wait_send()
     wait_bytes(slots_in.at[pl.ds(0, n_tile - 1)], many_send.at[0])
     wait_bytes(column.at[pl.ds(0, n_grp - 1)], many_send.at[1])
-    wait_bytes(part_in.at[pl.ds(0, n_tile - 1)], many_send.at[2])
-    wait_bytes(sum_in.at[pl.ds(0, n_grp - 1)], many_send.at[3])
+    wait_bytes(part_in.at[pl.ds(1, len(plane_offsets))], many_send.at[2])
+    wait_bytes(sum_in.at[pl.ds(1, len(line_offsets))], many_send.at[3])
     increment_copy.wait()
     probe_copy.wait()
 
@@ -399,7 +462,7 @@
     slots = pixel_los.shape[-1]
     panel_rows = panels.shape[1]
     vmem = pl.BlockSpec(memory_space=pltpu.VMEM)
-    anywhere = pl.BlockSpec(memory_space=pl.ANY)
+    hbm = pl.BlockSpec(memory_space=pltpu.HBM)
     wide = 64 + 2 * HALO
     increment, probe, coefficients = pl.pallas_call(
         functools.partial(kernel, n_grp, n_tile),
@@ -408,13 +471,21 @@
             jax.ShapeDtypeStruct((64, LANES), F32),
             jax.ShapeDtypeStruct((1, LANES), F32),
         ),
-        in_specs=[vmem] * 7 + [pl.BlockSpec(memory_space=pltpu.SMEM), anywhere],
-        out_specs=(anywhere, anywhere, vmem),
+        in_specs=[hbm] * 9,
+        out_specs=(hbm, hbm, vmem),
         scratch_shapes=[
+            pltpu.VMEM((2, 64, LANES), F32),
+            pltpu.VMEM((64, LANES), F32),
+            pltpu.VMEM((64, LANES), F32),
+            pltpu.VMEM((64, LANES), F32),
+            pltpu.VMEM((2, slots), F32),
+            pltpu.VMEM((1, slots), F32),
+            pltpu.VMEM((1, slots), jnp.int32),
+            pltpu.SMEM((1, n_tile), jnp.int32),
             pltpu.VMEM((4, wide, LANES), F32),
-            pltpu.VMEM((64, LANES), F32),
-            pltpu.VMEM((wide, LANES), F32),
-            pltpu.VMEM((wide, LANES), F32),
+            pltpu.VMEM((48, LANES), F32),
+            pltpu.VMEM((48, LANES), F32),
+            pltpu.VMEM((48, LANES), F32),
             pltpu.VMEM((n_tile // 2, 4, LANES), F32),
             pltpu.VMEM((n_tile, 4, LANES), F32),
             pltpu.VMEM((10, wide, 2 * LANES), F32),
@@ -422,37 +493,35 @@
             pltpu.VMEM((2, wide, 2 * LANES), F32),
             pltpu.VMEM((2, 64, LANES), F32),
             pltpu.VMEM((2, wide, LANES), F32),
-            pltpu.VMEM((64, LANES), F32),
-            pltpu.VMEM((wide, LANES), F32),
-            pltpu.VMEM((wide, LANES), F32),
+            pltpu.VMEM((32, LANES), F32),
+            pltpu.VMEM((32, LANES), F32),
+            pltpu.VMEM((32, LANES), F32),
             pltpu.VMEM((64, LANES), F32),
             pltpu.VMEM((64, LANES), BF16),
             pltpu.VMEM((n_grp, 64, LANES), BF16),
             pltpu.VMEM((8, panel_rows, LANES), BF16),
-            pltpu.VMEM((8, LANES), F32),
-            pltpu.VMEM((n_tile, 8, LANES), F32),
-            pltpu.VMEM((8, LANES), F32),
-            pltpu.VMEM((n_grp, 8, LANES), F32),
+            pltpu.VMEM((2 * n_grp, 1, LANES), F32),
+            pltpu.VMEM((n_tile // 2, 1, LANES), F32),
             pltpu.SemaphoreType.DMA((8,)),
             pltpu.SemaphoreType.DMA((8,)),
             pltpu.SemaphoreType.DMA((8,)),
             pltpu.SemaphoreType.DMA((8,)),
-            pltpu.SemaphoreType.DMA((3,)),
+            pltpu.SemaphoreType.DMA((11,)),
             pltpu.SemaphoreType.DMA((4,)),
             pltpu.SemaphoreType.DMA((4,)),
         ],
         compiler_params=pltpu.CompilerParams(
-            collective_id=0, has_side_effects=True, vmem_limit_bytes=24 * 1024 * 1024
+            collective_id=0, has_side_effects=True, vmem_limit_bytes=60 * 1024 * 1024
         ),
     )(
         base_velocity,
         viscosity,
         friction,
         friction_probe,
-        pixel_los.reshape(2, slots),
-        pixel_weight.reshape(1, slots),
-        pixel_cell.reshape(1, slots),
-        pixel_count.reshape(1, n_tile),
+        pixel_los,
+        pixel_weight,
+        pixel_cell,
+        pixel_count,
         panels,
     )
     return increment, probe, coefficients.reshape(LANES)[: 8 * n_grp]

time: 64.6 us -> 55.1 us (0.85)
  local copies, waits for them, and re-layouts: 9.22 us -> 4.04 us
  Pallas kernels: 54.1 us -> 50.2 us
    unnamed x21 -> x3, local copies, waits for them, and re-layouts: 9.22 us -> 4.04 us
    pallas_call x1, Pallas kernels: 54.1 us -> 50.2 us  [on_device(): pl.pallas_call(functools.partial(kernel, n_grp, n_tile), out_shape=(jax.S...]
where the time goes in v2:
time: 55.1 us; the launch traced here: 54.9 us
  Pallas kernels  50.2 us (91%)
  local copies, waits for them, and re-layouts  4.04 us (7%)
  between operations  0.64 us (1%)
    pallas_call x1, Pallas kernels, on_device(): pl.pallas_call(functools.partial(kernel, n_grp, n_tile), out_shape=(jax.S...  50.2 us
    unnamed x3, local copies, waits for them, and re-layouts  4.04 us

profile of v2, /device:TPU:1, one launch (start us, length us, event | category | flops | bytes accessed | tf_op | source)
XLA Modules:
  0.0 54.9 jit_solution(15215657574846894448)
XLA Ops:
  0.6 50.2 %shard_map.112 = (f32[2,64,128]{2,1,0:T(8,128)}, f32[64,128]{1,0:T(8,128)}, f32[1,128]{1,0:T(1,128)}) custom-call(f32[2,64,128]{2,1,0:T(8,128)} %base_velocity_in.1, f32[64,128]{1,0:T(8,128)} %viscosity_in.1, f32[64,128]{1,0:T(8,128)} %friction_in.1, f32[64,128]{1,0:T(8,128)} %friction_probe_in.1, f32[1,1,2,2048]{3,2,1,0:T(2,128)} %pixel_los_in.1, ...), custom_call_target="tpu_custom_call" | custom-call | tf_op jit(solution)/shard_map/pallas_call | solution.py:467
  50.8 1.5 %copy.15 = f32[2,64,128]{2,1,0:T(8,128)} copy(f32[2,64,128]{2,1,0:T(8,128)} %get-tuple-element.12) | data formatting | bytes 131072
  52.3 1.4 %copy.16 = f32[64,128]{1,0:T(8,128)} copy(f32[64,128]{1,0:T(8,128)} %get-tuple-element.13) | data formatting | bytes 65536
  53.7 1.2 %copy.17 = f32[128]{0:T(128)} copy(f32[128]{0:T(128)} %bitcast.1) | data formatting | bytes 1024

commit v3 on v2

--- a/solution.py
+++ b/solution.py
@@ -111,15 +111,22 @@
     side2_r,
     side2_l,
     probe_stage,
-    low_stage,
+    early_stage,
+    early_in,
+    late_stage,
+    late_in,
     column,
     panel_buf,
+    panel_ext,
+    panel_rim,
     part_in,
     sum_in,
     halo_send,
     halo_recv,
     halo2_send,
     halo2_recv,
+    rim_send,
+    rim_recv,
     local_sem,
     many_send,
     many_recv,
@@ -171,7 +178,8 @@
     barrier = pltpu.get_barrier_semaphore()
     corners = [(a, b) for a in (up, down) for b in (left, right)]
     across = [plane_peer(*p) for p in plane_offsets if p[1] % 2]
-    peers = [grp_peer(*p) for p in grp_offsets] + corners + across + [tile_peer(*p) for p in tile_offsets if p != (0, 2)]
+    peers = corners + [(up, t), (down, t), (g, left), (g, right)]
+    peers += [grp_peer(*p) for p in grp_offsets] + across + [tile_peer(*p) for p in tile_offsets if p != (0, 2)]
     for peer in peers:
         pl.semaphore_signal(barrier, inc=1, device_id=peer, device_id_type=MESH)
 
@@ -179,7 +187,7 @@
         pltpu.make_async_copy(a, b, local_sem.at[3 + index])
         for index, (a, b) in enumerate(
             [
-                (base_velocity_in, base_velocity),
+                (base_velocity_in, base_velocity.at[:, pl.ds(HALO, 64)]),
                 (viscosity_in, viscosity),
                 (friction_in, friction),
                 (friction_probe_in, friction_probe),
@@ -198,8 +206,8 @@
 
     for load in loads[:4]:
         load.wait()
-    bvx = base_velocity[0]
-    bvy = base_velocity[1]
+    bvx = base_velocity[0, HALO : HALO + 64]
+    bvy = base_velocity[1, HALO : HALO + 64]
     fp = friction_probe[...]
     own = (viscosity[...], friction[...], -(fp * bvx), -(fp * bvy))
     for index in range(4):
@@ -229,6 +237,16 @@
 
     pl.semaphore_wait(barrier, len(peers))
 
+    def remote(src_ref, dst_ref, send_sem, recv_sem, peer):
+        return pltpu.make_async_remote_copy(
+            src_ref=src_ref,
+            dst_ref=dst_ref,
+            send_sem=send_sem,
+            recv_sem=recv_sem,
+            device_id=peer,
+            device_id_type=MESH,
+        )
+
     def rim_copies(block, packed, from_right, from_left, send, recv):
         first, last = pl.ds(HALO, HALO), pl.ds(64, HALO)
         above, below = pl.ds(0, HALO), pl.ds(64 + HALO, HALO)
@@ -244,17 +262,7 @@
             (packed.at[middle], from_right.at[middle], (g, left)),
             (packed.at[middle], from_left.at[middle], (g, right)),
         ]
-        return [
-            pltpu.make_async_remote_copy(
-                src_ref=a,
-                dst_ref=b,
-                send_sem=send.at[index],
-                recv_sem=recv.at[index],
-                device_id=target,
-                device_id_type=MESH,
-            )
-            for index, (a, b, target) in enumerate(moves)
-        ]
+        return [remote(a, b, send.at[index], recv.at[index], peer) for index, (a, b, peer) in enumerate(moves)]
 
     def wait_bytes(ref, sem):
         pltpu.make_async_copy(ref, ref, sem).wait()
@@ -262,16 +270,19 @@
     copies = rim_copies(ext, pack, side_r, side_l, halo_send, halo_recv)
     for copy in copies:
         copy.start()
+    first, last = pl.ds(HALO, HALO), pl.ds(64, HALO)
+    above, below = pl.ds(0, HALO), pl.ds(64 + HALO, HALO)
+    velocity_rims = [
+        remote(base_velocity.at[:, first], base_velocity.at[:, below], rim_send.at[0], rim_recv.at[0], (up, t)),
+        remote(base_velocity.at[:, last], base_velocity.at[:, above], rim_send.at[1], rim_recv.at[1], (down, t)),
+    ]
+    for copy in velocity_rims:
+        copy.start()
 
     for dz, flip in tile_offsets:
         peer = tile_peer(dz, flip)
-        pltpu.make_async_remote_copy(
-            src_ref=slots_out.at[lax.div(peer[1], 2)],
-            dst_ref=slots_in.at[4 * dz + flip],
-            send_sem=many_send.at[0],
-            recv_sem=many_recv.at[0],
-            device_id=peer,
-            device_id_type=MESH,
+        remote(
+            slots_out.at[lax.div(peer[1], 2)], slots_in.at[4 * dz + flip], many_send.at[0], many_recv.at[0], peer
         ).start()
     slots_in[0] = slots_out[lax.div(t, 2)]
 
@@ -282,16 +293,20 @@
     lane = lane_of((rows, LANES))
     row = row_of((rows, LANES))
 
+    def merge(from_right, from_left):
+        return jnp.where(lax.rem(lane_of(from_right.shape), 16) >= 8, from_right, from_left)
+
+    def beside(merged, index):
+        return pltpu.roll(merged, LANES - 16 * index - 8, 1)
+
     def widen(block, from_right, from_left):
-        merged = jnp.where(lax.rem(lane_of(from_right.shape), 16) >= 8, from_right[...], from_left[...])
+        merged = merge(from_right[...], from_left[...])
         high = merged.shape[0] - 16
         middle = unfold_rows(merged[8 : 8 + high], 2 * high)
         merged = jnp.concatenate([merged[0:8], middle, merged[8 + high :]], axis=0)
-        fields = []
-        for index in range(block.shape[0]):
-            beside = pltpu.roll(merged, LANES - 16 * index - 8, 1)
-            fields.append(jnp.concatenate([block[index], beside], axis=1))
-        return fields
+        return [
+            jnp.concatenate([block[index], beside(merged, index)], axis=1) for index in range(block.shape[0])
+        ]
 
     v, fr, sx, sy = widen(ext, side_r, side_l)
     row_inside = ((row >= HALO) | (g > 0)) & ((row < HALO + 64) | (g < n_grp - 1))
@@ -336,9 +351,13 @@
         field[0] = coef[8] * src[0]
         field[1] = coef[9] * src[1]
         lax.fori_loop(1, SWEEPS, sweep, 0)
-        return field[0, HALO : HALO + 64, :LANES], field[1, HALO : HALO + 64, :LANES]
-
-    inc_x, inc_y = relax()
+
+    def probe_of(at):
+        return -(base_velocity[0, at] * field[0, at, :LANES] + base_velocity[1, at] * field[1, at, :LANES])
+
+    own_rows = slice(HALO, HALO + 64)
+    relax()
+    inc_x, inc_y = field[0, own_rows, :LANES], field[1, own_rows, :LANES]
     inc_stage[0] = inc_x
     inc_stage[1] = inc_y
     increment_copy = pltpu.make_async_copy(inc_stage, increment_out, local_sem.at[1])
@@ -388,44 +407,91 @@
     pack2[8:24] = fold_rows(packed2, 32)
     pack2[24:32] = packed2[56:64]
     copies2 = rim_copies(ext2, pack2, side2_r, side2_l, halo2_send, halo2_recv)
-    for copy in copies2:
+    for copy in copies2[6:] + copies2[:6]:
         copy.start()
-    for copy in copies2:
+
+    for index in range(2):
+        src[index] = jnp.zeros((rows, 2 * LANES), F32)
+        src[index, own_rows, :LANES] = adjoint[index]
+    relax()
+    for copy in velocity_rims:
         copy.wait_recv()
-    sx2, sy2 = widen(ext2, side2_r, side2_l)
-    src[0] = sx2
-    src[1] = sy2
-    mult_x, mult_y = relax()
-
-    probe = -(base_velocity[0] * mult_x + base_velocity[1] * mult_y)
-    probe_low = probe.astype(BF16)
-    low_stage[...] = probe_low
-    column[g] = probe_low
-
+    everything = slice(0, rows)
+    part = probe_of(everything).astype(BF16)
+    early_stage[...] = part
+    early_in[g] = part
     for offset in grp_offsets:
-        pltpu.make_async_remote_copy(
-            src_ref=low_stage,
-            dst_ref=column.at[g],
-            send_sem=many_send.at[1],
-            recv_sem=many_recv.at[1],
-            device_id=grp_peer(*offset),
-            device_id_type=MESH,
-        ).start()
-    probe_stage[...] = probe
+        remote(early_stage, early_in.at[g], many_send.at[1], many_recv.at[1], grp_peer(*offset)).start()
+
+    panel_copy.wait()
+    panel_ext[0:HALO] = jnp.zeros((HALO, LANES), F32)
+    panel_ext[HALO + 64 * n_grp :] = jnp.zeros((HALO, LANES), F32)
+    fold_lane = lane_of((16, LANES))
+
+    def fold_late(block, start):
+        folded = jnp.zeros((16, LANES), F32)
+        for j in range(rows // 16):
+            moved = pltpu.roll(block[start + 16 * j : start + 16 * j + 16, :], 16 * j + 8, 1)
+            here = (fold_lane >= 16 * j) & (fold_lane < 16 * j + 16)
+            folded = jnp.where(here, moved, folded)
+        return folded
+
+    def fold_panel(k, carry):
+        panel_ext[HALO : HALO + 64 * n_grp] = panel_buf[k].astype(F32)
+        for block in range(n_grp):
+            panel_rim[k, block] = fold_late(panel_ext, 64 * block)
+        return carry
+
+    lax.fori_loop(0, 8, fold_panel, 0)
+
+    for copy in copies2[6:]:
+        copy.wait_recv()
+    middle = unfold_rows(merge(side2_r[8:24], side2_l[8:24]), 32)
+    for index in range(2):
+        src[index, own_rows, LANES:] = beside(middle, index)
+    relax()
+    late = fold_late(probe_of(everything), 0).astype(BF16)
+    late_stage[...] = late
+    late_in[g] = late
+    for offset in grp_offsets:
+        remote(late_stage, late_in.at[g], many_send.at[2], many_recv.at[2], grp_peer(*offset)).start()
+
+    for copy in copies2[:6]:
+        copy.wait_recv()
+    for at, edge in ((slice(0, 8), slice(0, 8)), (slice(64 + HALO, rows), slice(24, 32))):
+        merged = merge(side2_r[edge], side2_l[edge])
+        for index in range(2):
+            src[index, at, :LANES] = ext2[index, at]
+            src[index, at, LANES:] = beside(merged, index)
+    relax()
+    probe_stage[...] = probe_of(own_rows)
     probe_copy = pltpu.make_async_copy(probe_stage, probe_out, local_sem.at[2])
     probe_copy.start()
-    panel_copy.wait()
-    wait_bytes(column.at[pl.ds(0, n_grp - 1)], many_recv.at[1])
+
+    wait_bytes(early_in.at[pl.ds(0, n_grp - 1)], many_recv.at[1])
+    column[...] = jnp.zeros_like(column)
+    part_lane = lane_of((rows, LANES))
+    is_middle = (part_lane >= HALO) & (part_lane < LANES - HALO)
+    for block in range(n_grp):
+        at = slice(64 * block, 64 * block + rows)
+        column[at] += jnp.where(is_middle, early_in[block].astype(F32), 0.0)
 
     def project(block, sums):
-        values = column[block].astype(F32)
         start = pl.multiple_of(block * 64, 64)
+        values = column[pl.ds(start + HALO, 64), :]
         return tuple(
             total + jnp.sum((panel_buf[k, pl.ds(start, 64), :].astype(F32) * values).reshape(8, 8, LANES), axis=0)
             for k, total in enumerate(sums)
         )
 
     sums = lax.fori_loop(0, n_grp, project, tuple(jnp.zeros((8, LANES), F32) for _ in range(8)))
+    wait_bytes(late_in.at[pl.ds(0, n_grp - 1)], many_recv.at[2])
+    sums = list(sums)
+    for block in range(n_grp):
+        late = late_in[block].astype(F32)
+        for k in range(8):
+            product = panel_rim[k, block] * late
+            sums[k] = sums[k] + product[0:8] + product[8:16]
     partial = jnp.concatenate([jnp.sum(s, axis=0, keepdims=True) for s in sums], axis=0)
     partial = jnp.sum(partial, axis=1, keepdims=True)
     mine = lane_of((8, LANES)) == 8 * g + row_of((8, LANES))
@@ -434,26 +500,22 @@
     def sum_over(value, landing, offsets, peer, index):
         landing[0] = value
         for slot, offset in enumerate(offsets, 1):
-            pltpu.make_async_remote_copy(
-                src_ref=landing.at[0],
-                dst_ref=landing.at[slot],
-                send_sem=many_send.at[index],
-                recv_sem=many_recv.at[index],
-                device_id=peer(*offset),
-                device_id_type=MESH,
+            remote(
+                landing.at[0], landing.at[slot], many_send.at[index], many_recv.at[index], peer(*offset)
             ).start()
         wait_bytes(landing.at[pl.ds(1, len(offsets))], many_recv.at[index])
         return jnp.sum(landing[...], axis=0)
 
-    plane_sum = sum_over(placed, part_in, plane_offsets, plane_peer, 2)
-    coef_out[...] = sum_over(plane_sum, sum_in, line_offsets, line_peer, 3)
-
-    for copy in copies + copies2:
+    plane_sum = sum_over(placed, part_in, plane_offsets, plane_peer, 3)
+    coef_out[...] = sum_over(plane_sum, sum_in, line_offsets, line_peer, 4)
+
+    for copy in copies + velocity_rims + copies2:
         copy.wait_send()
     wait_bytes(slots_in.at[pl.ds(0, n_tile - 1)], many_send.at[0])
-    wait_bytes(column.at[pl.ds(0, n_grp - 1)], many_send.at[1])
-    wait_bytes(part_in.at[pl.ds(1, len(plane_offsets))], many_send.at[2])
-    wait_bytes(sum_in.at[pl.ds(1, len(line_offsets))], many_send.at[3])
+    wait_bytes(early_in.at[pl.ds(0, n_grp - 1)], many_send.at[1])
+    wait_bytes(late_in.at[pl.ds(0, n_grp - 1)], many_send.at[2])
+    wait_bytes(part_in.at[pl.ds(1, len(plane_offsets))], many_send.at[3])
+    wait_bytes(sum_in.at[pl.ds(1, len(line_offsets))], many_send.at[4])
     increment_copy.wait()
     probe_copy.wait()
 
@@ -474,7 +536,7 @@
         in_specs=[hbm] * 9,
         out_specs=(hbm, hbm, vmem),
         scratch_shapes=[
-            pltpu.VMEM((2, 64, LANES), F32),
+            pltpu.VMEM((2, wide, LANES), F32),
             pltpu.VMEM((64, LANES), F32),
             pltpu.VMEM((64, LANES), F32),
             pltpu.VMEM((64, LANES), F32),
@@ -497,32 +559,44 @@
             pltpu.VMEM((32, LANES), F32),
             pltpu.VMEM((32, LANES), F32),
             pltpu.VMEM((64, LANES), F32),
-            pltpu.VMEM((64, LANES), BF16),
-            pltpu.VMEM((n_grp, 64, LANES), BF16),
+            pltpu.VMEM((wide, LANES), BF16),
+            pltpu.VMEM((n_grp, wide, LANES), BF16),
+            pltpu.VMEM((16, LANES), BF16),
+            pltpu.VMEM((n_grp, 16, LANES), BF16),
+            pltpu.VMEM((panel_rows + 2 * HALO, LANES), F32),
             pltpu.VMEM((8, panel_rows, LANES), BF16),
+            pltpu.VMEM((panel_rows + 2 * HALO, LANES), F32),
+            pltpu.VMEM((8, n_grp, 16, LANES), F32),
             pltpu.VMEM((2 * n_grp, 1, LANES), F32),
             pltpu.VMEM((n_tile // 2, 1, LANES), F32),
             pltpu.SemaphoreType.DMA((8,)),
             pltpu.SemaphoreType.DMA((8,)),
             pltpu.SemaphoreType.DMA((8,)),
             pltpu.SemaphoreType.DMA((8,)),
+            pltpu.SemaphoreType.DMA((2,)),
+            pltpu.SemaphoreType.DMA((2,)),
             pltpu.SemaphoreType.DMA((11,)),
-            pltpu.SemaphoreType.DMA((4,)),
-            pltpu.SemaphoreType.DMA((4,)),
+            pltpu.SemaphoreType.DMA((5,)),
+            pltpu.SemaphoreType.DMA((5,)),
         ],
         compiler_params=pltpu.CompilerParams(
-            collective_id=0, has_side_effects=True, vmem_limit_bytes=60 * 1024 * 1024
+            collective_id=0, has_side_effects=True, vmem_limit_bytes=24 * 1024 * 1024
         ),
     )(
-        base_velocity,
-        viscosity,
-        friction,
-        friction_probe,
-        pixel_los,
-        pixel_weight,
-        pixel_cell,
-        pixel_count,
-        panels,
+        *(
+            pltpu.with_memory_space_constraint(a, pltpu.HBM)
+            for a in (
+                base_velocity,
+                viscosity,
+                friction,
+                friction_probe,
+                pixel_los,
+                pixel_weight,
+                pixel_cell,
+                pixel_count,
+                panels,
+            )
+        )
     )
     return increment, probe, coefficients.reshape(LANES)[: 8 * n_grp]
 

time: 55.1 us -> 51.1 us (0.927)
  local copies, waits for them, and re-layouts: 4.04 us -> 1.76 us
  Pallas kernels: 50.2 us -> 48.6 us
    unnamed x3, local copies, waits for them, and re-layouts: 4.04 us -> 1.76 us
    pallas_call x1, Pallas kernels: 50.2 us -> 48.6 us  [on_device(): pl.pallas_call(functools.partial(kernel, n_grp, n_tile), out_shape=(jax.S...]
where the time goes in v3:
time: 51.1 us; the launch traced here: 51 us
  Pallas kernels  48.6 us (95%)
  local copies, waits for them, and re-layouts  1.76 us (3%)
  between operations  0.64 us (1%)
    pallas_call x1, Pallas kernels, on_device(): pl.pallas_call(functools.partial(kernel, n_grp, n_tile), out_shape=(jax.S...  48.6 us
    unnamed x3, local copies, waits for them, and re-layouts  1.76 us

profile of v3, /device:TPU:1, one launch (start us, length us, event | category | flops | bytes accessed | tf_op | source)
XLA Modules:
  0.0 51.0 jit_solution(10628637399820452072)
XLA Ops:
  0.6 48.6 %shard_map.112 = (f32[2,64,128]{2,1,0:T(8,128)S(1)}, f32[64,128]{1,0:T(8,128)S(1)}, f32[1,128]{1,0:T(1,128)S(1)}) custom-call(f32[2,64,128]{2,1,0:T(8,128)} %base_velocity_in.1, f32[64,128]{1,0:T(8,128)} %viscosity_in.1, f32[64,128]{1,0:T(8,128)} %friction_in.1, f32[64,128]{1,0:T(8,128)} %friction_probe_in.1, f32[1,1,2,2048]{3,2,1,0:T(2,128)} %pixel_los_in.1, ...), custom_call_target="tpu_custom_call" | custom-call | tf_op jit(solution)/shard_map/pallas_call | solution.py:529
  49.2 0.6 %copy.15 = f32[2,64,128]{2,1,0:T(8,128)} copy(f32[2,64,128]{2,1,0:T(8,128)S(1)} %get-tuple-element.12) | data formatting | bytes 131072
  49.8 0.6 %copy.16 = f32[64,128]{1,0:T(8,128)} copy(f32[64,128]{1,0:T(8,128)S(1)} %get-tuple-element.13) | data formatting | bytes 65536
  50.5 0.5 %copy.17 = f32[128]{0:T(128)} copy(f32[128]{0:T(128)S(1)} %bitcast.1) | data formatting | bytes 1024

commit v4 on v3

--- a/solution.py
+++ b/solution.py
@@ -127,6 +127,8 @@
     halo2_recv,
     rim_send,
     rim_recv,
+    hand_send,
+    hand_recv,
     local_sem,
     many_send,
     many_recv,
@@ -420,7 +422,11 @@
     part = probe_of(everything).astype(BF16)
     early_stage[...] = part
     early_in[g] = part
-    for offset in grp_offsets:
+    opposite = grp_peer(0, y_size // 2)
+    handed_on = [(dx, 0) for dx in range(1, x_size)]
+    direct = [offset for offset in grp_offsets if offset[1] != y_size // 2]
+    remote(early_stage, early_in.at[g], hand_send.at[0], hand_recv.at[0], opposite).start()
+    for offset in direct:
         remote(early_stage, early_in.at[g], many_send.at[1], many_recv.at[1], grp_peer(*offset)).start()
 
     panel_copy.wait()
@@ -456,6 +462,12 @@
     for offset in grp_offsets:
         remote(late_stage, late_in.at[g], many_send.at[2], many_recv.at[2], grp_peer(*offset)).start()
 
+    wait_bytes(early_in.at[0], hand_recv.at[0])
+    for offset in handed_on:
+        remote(
+            early_in.at[opposite[0]], early_in.at[opposite[0]], hand_send.at[1], hand_recv.at[1], grp_peer(*offset)
+        ).start()
+
     for copy in copies2[:6]:
         copy.wait_recv()
     for at, edge in ((slice(0, 8), slice(0, 8)), (slice(64 + HALO, rows), slice(24, 32))):
@@ -468,7 +480,9 @@
     probe_copy = pltpu.make_async_copy(probe_stage, probe_out, local_sem.at[2])
     probe_copy.start()
 
-    wait_bytes(early_in.at[pl.ds(0, n_grp - 1)], many_recv.at[1])
+    wait_bytes(early_in.at[pl.ds(0, len(direct))], many_recv.at[1])
+    if handed_on:
+        wait_bytes(early_in.at[pl.ds(0, len(handed_on))], hand_recv.at[1])
     column[...] = jnp.zeros_like(column)
     part_lane = lane_of((rows, LANES))
     is_middle = (part_lane >= HALO) & (part_lane < LANES - HALO)
@@ -512,7 +526,10 @@
     for copy in copies + velocity_rims + copies2:
         copy.wait_send()
     wait_bytes(slots_in.at[pl.ds(0, n_tile - 1)], many_send.at[0])
-    wait_bytes(early_in.at[pl.ds(0, n_grp - 1)], many_send.at[1])
+    wait_bytes(early_in.at[pl.ds(0, len(direct))], many_send.at[1])
+    wait_bytes(early_in.at[0], hand_send.at[0])
+    if handed_on:
+        wait_bytes(early_in.at[pl.ds(0, len(handed_on))], hand_send.at[1])
     wait_bytes(late_in.at[pl.ds(0, n_grp - 1)], many_send.at[2])
     wait_bytes(part_in.at[pl.ds(1, len(plane_offsets))], many_send.at[3])
     wait_bytes(sum_in.at[pl.ds(1, len(line_offsets))], many_send.at[4])
@@ -575,6 +592,8 @@
             pltpu.SemaphoreType.DMA((8,)),
             pltpu.SemaphoreType.DMA((2,)),
             pltpu.SemaphoreType.DMA((2,)),
+            pltpu.SemaphoreType.DMA((2,)),
+            pltpu.SemaphoreType.DMA((2,)),
             pltpu.SemaphoreType.DMA((11,)),
             pltpu.SemaphoreType.DMA((5,)),
             pltpu.SemaphoreType.DMA((5,)),

time: 51.1 us -> 49.3 us (0.965)
  Pallas kernels: 48.6 us -> 46.8 us
    pallas_call x1, Pallas kernels: 48.6 us -> 46.8 us  [on_device(): pl.pallas_call(functools.partial(kernel, n_grp, n_tile), out_shape=(jax.S...]
where the time goes in v4:
time: 49.3 us; the launch traced here: 49.2 us
  Pallas kernels  46.8 us (95%)
  local copies, waits for them, and re-layouts  1.76 us (4%)
  between operations  0.64 us (1%)
    pallas_call x1, Pallas kernels, on_device(): pl.pallas_call(functools.partial(kernel, n_grp, n_tile), out_shape=(jax.S...  46.8 us
    unnamed x3, local copies, waits for them, and re-layouts  1.76 us

profile of v4, /device:TPU:1, one launch (start us, length us, event | category | flops | bytes accessed | tf_op | source)
XLA Modules:
  0.0 49.2 jit_solution(8554533503840935010)
XLA Ops:
  0.6 46.8 %shard_map.112 = (f32[2,64,128]{2,1,0:T(8,128)S(1)}, f32[64,128]{1,0:T(8,128)S(1)}, f32[1,128]{1,0:T(1,128)S(1)}) custom-call(f32[2,64,128]{2,1,0:T(8,128)} %base_velocity_in.1, f32[64,128]{1,0:T(8,128)} %viscosity_in.1, f32[64,128]{1,0:T(8,128)} %friction_in.1, f32[64,128]{1,0:T(8,128)} %friction_probe_in.1, f32[1,1,2,2048]{3,2,1,0:T(2,128)} %pixel_los_in.1, ...), custom_call_target="tpu_custom_call" | custom-call | tf_op jit(solution)/shard_map/pallas_call | solution.py:546
  47.4 0.6 %copy.15 = f32[2,64,128]{2,1,0:T(8,128)} copy(f32[2,64,128]{2,1,0:T(8,128)S(1)} %get-tuple-element.12) | data formatting | bytes 131072
  48.0 0.6 %copy.16 = f32[64,128]{1,0:T(8,128)} copy(f32[64,128]{1,0:T(8,128)S(1)} %get-tuple-element.13) | data formatting | bytes 65536
  48.7 0.5 %copy.17 = f32[128]{0:T(128)} copy(f32[128]{0:T(128)S(1)} %bitcast.1) | data formatting | bytes 1024

commit v5 on v4

--- a/solution.py
+++ b/solution.py
@@ -105,12 +105,11 @@
     coef,
     src,
     field,
-    inc_stage,
+    other,
     ext2,
     pack2,
     side2_r,
     side2_l,
-    probe_stage,
     early_stage,
     early_in,
     late_stage,
@@ -186,7 +185,7 @@
         pl.semaphore_signal(barrier, inc=1, device_id=peer, device_id_type=MESH)
 
     loads = [
-        pltpu.make_async_copy(a, b, local_sem.at[3 + index])
+        pltpu.make_async_copy(a, b, local_sem.at[1 + index])
         for index, (a, b) in enumerate(
             [
                 (base_velocity_in, base_velocity.at[:, pl.ds(HALO, 64)]),
@@ -329,41 +328,77 @@
     inv_x = jnp.where(inside, RELAX / jnp.where(inside, diag_x, 1.0), 0.0)
     inv_y = jnp.where(inside, RELAX / jnp.where(inside, diag_y, 1.0), 0.0)
     for index, term in enumerate((east, west, north, south, node_pp, node_mp, node_pm, node_mm, inv_x, inv_y)):
-        coef[index] = term
-    src[0] = sx
-    src[1] = sy
-
-    def sweep(_, carry):
-        cx, cy = field[0], field[1]
-        ux, uy = row_next(cx), row_next(cy)
-        dx, dy = row_prev(cx), row_prev(cy)
-        e, w, n, s = coef[0], coef[1], coef[2], coef[3]
-        pp, mp, pm, mm = coef[4], coef[5], coef[6], coef[7]
-        ax = 2.0 * (e * ux + w * dx)
-        ax += col_next(s * cx + (pm * uy - mm * dy))
-        ax += col_prev(n * cx + (mp * dy - pp * uy))
-        ay = e * uy + w * dy
-        ay += col_next(2.0 * (s * cy) + (pm * ux - mm * dx))
-        ay += col_prev(2.0 * (n * cy) + (mp * dx - pp * ux))
-        field[0] = (1.0 - RELAX) * cx + coef[8] * (src[0] + ax)
-        field[1] = (1.0 - RELAX) * cy + coef[9] * (src[1] + ay)
+        coef[index, 0] = term[:, :LANES]
+        coef[index, 1] = term[:, LANES:]
+    for index, term in enumerate((sx, sy)):
+        src[index, 0] = term[:, :LANES]
+        src[index, 1] = term[:, LANES:]
+    for buffer in (field, other):
+        buffer[:, :, 0:HALO] = jnp.zeros((2, 2, HALO, LANES), F32)
+        buffer[:, :, HALO + rows :] = jnp.zeros((2, 2, HALO, LANES), F32)
+    tile_lane = lane_of((8, LANES))
+    at_last, at_first = tile_lane == LANES - 1, tile_lane == 0
+
+    def pair_next(pair):
+        own, rim = (pltpu.roll(a, LANES - 1, 1) for a in pair)
+        return jnp.where(at_last, rim, own), jnp.where(at_last, own, rim)
+
+    def pair_prev(pair):
+        own, rim = (pltpu.roll(a, 1, 1) for a in pair)
+        return jnp.where(at_first, rim, own), jnp.where(at_first, own, rim)
+
+    def sweep(now, later):
+        for tile in range(rows // 8):
+            at = slice(8 * tile, 8 * tile + 8)
+            inner = slice(8 * tile + HALO, 8 * tile + HALO + 8)
+            after = slice(8 * tile + HALO + 1, 8 * tile + HALO + 9)
+            before = slice(8 * tile + HALO - 1, 8 * tile + HALO + 7)
+            axial, forward, backward, centre = ([], []), ([], []), ([], []), ([], [])
+            for part in range(2):
+                e, w, n, s, pp, mp, pm, mm = (coef[index, part, at] for index in range(8))
+                cx, cy = now[0, part, inner], now[1, part, inner]
+                ux, uy = now[0, part, after], now[1, part, after]
+                dx, dy = now[0, part, before], now[1, part, before]
+                ax = e * ux + w * dx
+                cy2 = cy + cy
+                axial[0].append(ax + ax)
+                axial[1].append(e * uy + w * dy)
+                forward[0].append(s * cx + (pm * uy - mm * dy))
+                forward[1].append(s * cy2 + (pm * ux - mm * dx))
+                backward[0].append(n * cx + (mp * dy - pp * uy))
+                backward[1].append(n * cy2 + (mp * dx - pp * ux))
+                centre[0].append(cx)
+                centre[1].append(cy)
+            for index in range(2):
+                ahead, behind = pair_next(forward[index]), pair_prev(backward[index])
+                for part in range(2):
+                    total = src[index, part, at] + axial[index][part] + (ahead[part] + behind[part])
+                    later[index, part, inner] = (1.0 - RELAX) * centre[index][part] + (
+                        coef[8 + index, part, at] * total
+                    )
+
+    def two_sweeps(_, carry):
+        sweep(other, field)
+        sweep(field, other)
         return carry
 
     def relax():
-        field[0] = coef[8] * src[0]
-        field[1] = coef[9] * src[1]
-        lax.fori_loop(1, SWEEPS, sweep, 0)
+        for index in range(2):
+            other[index, :, HALO : HALO + rows] = coef[8 + index] * src[index]
+        lax.fori_loop(0, (SWEEPS - 2) // 2, two_sweeps, 0)
+        sweep(other, field)
+
+    def solved(index, at):
+        return field[index, 0, at.start + HALO : at.stop + HALO]
 
     def probe_of(at):
-        return -(base_velocity[0, at] * field[0, at, :LANES] + base_velocity[1, at] * field[1, at, :LANES])
+        return -(base_velocity[0, at] * solved(0, at) + base_velocity[1, at] * solved(1, at))
 
     own_rows = slice(HALO, HALO + 64)
     relax()
-    inc_x, inc_y = field[0, own_rows, :LANES], field[1, own_rows, :LANES]
-    inc_stage[0] = inc_x
-    inc_stage[1] = inc_y
-    increment_copy = pltpu.make_async_copy(inc_stage, increment_out, local_sem.at[1])
-    increment_copy.start()
+    inc_x, inc_y = solved(0, own_rows), solved(1, own_rows)
+    increment_out[0] = inc_x
+    increment_out[1] = inc_y
 
     wait_bytes(slots_in.at[pl.ds(0, n_tile - 1)], many_recv.at[0])
 
@@ -413,8 +448,8 @@
         copy.start()
 
     for index in range(2):
-        src[index] = jnp.zeros((rows, 2 * LANES), F32)
-        src[index, own_rows, :LANES] = adjoint[index]
+        src[index] = jnp.zeros((2, rows, LANES), F32)
+        src[index, 0, own_rows] = adjoint[index]
     relax()
     for copy in velocity_rims:
         copy.wait_recv()
@@ -454,7 +489,7 @@
         copy.wait_recv()
     middle = unfold_rows(merge(side2_r[8:24], side2_l[8:24]), 32)
     for index in range(2):
-        src[index, own_rows, LANES:] = beside(middle, index)
+        src[index, 1, own_rows] = beside(middle, index)
     relax()
     late = fold_late(probe_of(everything), 0).astype(BF16)
     late_stage[...] = late
@@ -473,12 +508,10 @@
     for at, edge in ((slice(0, 8), slice(0, 8)), (slice(64 + HALO, rows), slice(24, 32))):
         merged = merge(side2_r[edge], side2_l[edge])
         for index in range(2):
-            src[index, at, :LANES] = ext2[index, at]
-            src[index, at, LANES:] = beside(merged, index)
+            src[index, 0, at] = ext2[index, at]
+            src[index, 1, at] = beside(merged, index)
     relax()
-    probe_stage[...] = probe_of(own_rows)
-    probe_copy = pltpu.make_async_copy(probe_stage, probe_out, local_sem.at[2])
-    probe_copy.start()
+    probe_out[...] = probe_of(own_rows)
 
     wait_bytes(early_in.at[pl.ds(0, len(direct))], many_recv.at[1])
     if handed_on:
@@ -533,8 +566,17 @@
     wait_bytes(late_in.at[pl.ds(0, n_grp - 1)], many_send.at[2])
     wait_bytes(part_in.at[pl.ds(1, len(plane_offsets))], many_send.at[3])
     wait_bytes(sum_in.at[pl.ds(1, len(line_offsets))], many_send.at[4])
-    increment_copy.wait()
-    probe_copy.wait()
+
+
+def hand_out(a, b, c, a_out, b_out, c_out, sems):
+    copies = [
+        pltpu.make_async_copy(src, dst, sems.at[index])
+        for index, (src, dst) in enumerate(((a, a_out), (b, b_out), (c, c_out)))
+    ]
+    for copy in copies:
+        copy.start()
+    for copy in copies:
+        copy.wait()
 
 
 def on_device(n_grp, n_tile, base_velocity, viscosity, friction, friction_probe, pixel_los, pixel_weight, pixel_cell, pixel_count, panels):
@@ -546,12 +588,12 @@
     increment, probe, coefficients = pl.pallas_call(
         functools.partial(kernel, n_grp, n_tile),
         out_shape=(
-            jax.ShapeDtypeStruct((2, 64, LANES), F32),
-            jax.ShapeDtypeStruct((64, LANES), F32),
-            jax.ShapeDtypeStruct((1, LANES), F32),
+            pltpu.VMEM((2, 64, LANES), F32),
+            pltpu.VMEM((64, LANES), F32),
+            pltpu.VMEM((1, LANES), F32),
         ),
         in_specs=[hbm] * 9,
-        out_specs=(hbm, hbm, vmem),
+        out_specs=(vmem, vmem, vmem),
         scratch_shapes=[
             pltpu.VMEM((2, wide, LANES), F32),
             pltpu.VMEM((64, LANES), F32),
@@ -567,15 +609,14 @@
             pltpu.VMEM((48, LANES), F32),
             pltpu.VMEM((n_tile // 2, 4, LANES), F32),
             pltpu.VMEM((n_tile, 4, LANES), F32),
-            pltpu.VMEM((10, wide, 2 * LANES), F32),
-            pltpu.VMEM((2, wide, 2 * LANES), F32),
-            pltpu.VMEM((2, wide, 2 * LANES), F32),
-            pltpu.VMEM((2, 64, LANES), F32),
+            pltpu.VMEM((10, 2, wide, LANES), F32),
+            pltpu.VMEM((2, 2, wide, LANES), F32),
+            pltpu.VMEM((2, 2, wide + 2 * HALO, LANES), F32),
+            pltpu.VMEM((2, 2, wide + 2 * HALO, LANES), F32),
             pltpu.VMEM((2, wide, LANES), F32),
             pltpu.VMEM((32, LANES), F32),
             pltpu.VMEM((32, LANES), F32),
             pltpu.VMEM((32, LANES), F32),
-            pltpu.VMEM((64, LANES), F32),
             pltpu.VMEM((wide, LANES), BF16),
             pltpu.VMEM((n_grp, wide, LANES), BF16),
             pltpu.VMEM((16, LANES), BF16),
@@ -594,7 +635,7 @@
             pltpu.SemaphoreType.DMA((2,)),
             pltpu.SemaphoreType.DMA((2,)),
             pltpu.SemaphoreType.DMA((2,)),
-            pltpu.SemaphoreType.DMA((11,)),
+            pltpu.SemaphoreType.DMA((9,)),
             pltpu.SemaphoreType.DMA((5,)),
             pltpu.SemaphoreType.DMA((5,)),
         ],
@@ -617,6 +658,17 @@
             )
         )
     )
+    increment, probe, coefficients = pl.pallas_call(
+        hand_out,
+        out_shape=(
+            jax.ShapeDtypeStruct((2, 64, LANES), F32),
+            jax.ShapeDtypeStruct((64, LANES), F32),
+            jax.ShapeDtypeStruct((1, LANES), F32),
+        ),
+        in_specs=[vmem] * 3,
+        out_specs=(hbm, hbm, hbm),
+        scratch_shapes=[pltpu.SemaphoreType.DMA((3,))],
+    )(*(pltpu.with_memory_space_constraint(a, pltpu.VMEM) for a in (increment, probe, coefficients)))
     return increment, probe, coefficients.reshape(LANES)[: 8 * n_grp]
 
 

time: 49.3 us -> 47.9 us (0.972)
  local copies, waits for them, and re-layouts: 1.76 us -> 0 us
    unnamed x3 -> x0, local copies, waits for them, and re-layouts: 1.76 us -> none
    pallas_call x1 -> x2, Pallas kernels: 46.8 us -> 47.1 us  [the longest x1 46.4 us: on_device(): pl.pallas_call(functools.partial(kernel, n_grp, n_tile), out_shape=(pltpu...]
where the time goes in v5:
time: 47.9 us; the launch traced here: 47.7 us
  Pallas kernels  47.1 us (98%)
  between operations  0.64 us (1%)
    pallas_call x1, Pallas kernels, on_device(): pl.pallas_call(functools.partial(kernel, n_grp, n_tile), out_shape=(pltpu...  46.4 us

profile of v5, /device:TPU:1, one launch (start us, length us, event | category | flops | bytes accessed | tf_op | source)
XLA Modules:
  0.0 47.7 jit_solution(10430202757313479124)
XLA Ops:
  0.6 46.4 %shard_map.112 = (f32[2,64,128]{2,1,0:T(8,128)S(1)}, f32[64,128]{1,0:T(8,128)S(1)}, f32[1,128]{1,0:T(1,128)S(1)}) custom-call(f32[2,64,128]{2,1,0:T(8,128)} %base_velocity_in.1, f32[64,128]{1,0:T(8,128)} %viscosity_in.1, f32[64,128]{1,0:T(8,128)} %friction_in.1, f32[64,128]{1,0:T(8,128)} %friction_probe_in.1, f32[1,1,2,2048]{3,2,1,0:T(2,128)} %pixel_los_in.1, ...), custom_call_target="tpu_custom_call" | custom-call | tf_op jit(solution)/shard_map/pallas_call | solution.py:588
  47.1 0.7 %shard_map.113 = (f32[2,64,128]{2,1,0:T(8,128)}, f32[64,128]{1,0:T(8,128)}, f32[1,128]{1,0:T(1,128)}) custom-call(f32[2,64,128]{2,1,0:T(8,128)S(1)} %get-tuple-element.9.a, f32[64,128]{1,0:T(8,128)S(1)} %get-tuple-element.10.b, f32[1,128]{1,0:T(1,128)S(1)} %get-tuple-element.11.c), custom_call_target="tpu_custom_call" | custom-call | tf_op jit(solution)/shard_map/pallas_call | solution.py:661

commit v6 on v5

--- a/solution.py
+++ b/solution.py
@@ -106,6 +106,10 @@
     src,
     field,
     other,
+    strip_coef,
+    strip_src,
+    strip,
+    strip_other,
     ext2,
     pack2,
     side2_r,
@@ -485,13 +489,59 @@
 
     lax.fori_loop(0, 8, fold_panel, 0)
 
+    near_left = (lane < 8) | (lane >= 120)
+    near_right = (lane >= 56) & (lane < 72)
+    for index in range(10):
+        left_strip = jnp.where(lane < 64, coef[index, 0], coef[index, 1])
+        right_strip = pltpu.roll(jnp.where(lane < 64, coef[index, 1], coef[index, 0]), 64, 1)
+        strip_coef[index] = jnp.where(near_left, left_strip, jnp.where(near_right, right_strip, 0.0))
+    strip_src[...] = jnp.zeros((2, rows, LANES), F32)
+    for buffer in (strip, strip_other):
+        buffer[...] = jnp.zeros((2, rows + 2 * HALO, LANES), F32)
+
+    def strip_sweep(now, later):
+        for tile in range(rows // 8):
+            at = slice(8 * tile, 8 * tile + 8)
+            inner = slice(8 * tile + HALO, 8 * tile + HALO + 8)
+            after = slice(8 * tile + HALO + 1, 8 * tile + HALO + 9)
+            before = slice(8 * tile + HALO - 1, 8 * tile + HALO + 7)
+            e, w, n, s, pp, mp, pm, mm = (strip_coef[index, at] for index in range(8))
+            cx, cy = now[0, inner], now[1, inner]
+            ux, uy = now[0, after], now[1, after]
+            dx, dy = now[0, before], now[1, before]
+            ax = e * ux + w * dx
+            cy2 = cy + cy
+            ax = ax + ax + (col_next(s * cx + (pm * uy - mm * dy)) + col_prev(n * cx + (mp * dy - pp * uy)))
+            ay = e * uy + w * dy
+            ay = ay + (col_next(s * cy2 + (pm * ux - mm * dx)) + col_prev(n * cy2 + (mp * dx - pp * ux)))
+            later[0, inner] = (1.0 - RELAX) * cx + strip_coef[8, at] * (strip_src[0, at] + ax)
+            later[1, inner] = (1.0 - RELAX) * cy + strip_coef[9, at] * (strip_src[1, at] + ay)
+
+    def two_strip_sweeps(_, carry):
+        strip_sweep(strip_other, strip)
+        strip_sweep(strip, strip_other)
+        return carry
+
     for copy in copies2[6:]:
         copy.wait_recv()
     middle = unfold_rows(merge(side2_r[8:24], side2_l[8:24]), 32)
+    rim_lane = lane_of((64, LANES))
     for index in range(2):
-        src[index, 1, own_rows] = beside(middle, index)
-    relax()
-    late = fold_late(probe_of(everything), 0).astype(BF16)
+        rim = beside(middle, index)
+        src[index, 1, own_rows] = rim
+        moved = jnp.where((rim_lane >= 64) & (rim_lane < 72), pltpu.roll(rim, 64, 1), 0.0)
+        strip_src[index, own_rows] = jnp.where(rim_lane >= 120, rim, moved)
+    for index in range(2):
+        strip_other[index, HALO : HALO + rows] = strip_coef[8 + index] * strip_src[index]
+    lax.fori_loop(0, (SWEEPS - 2) // 2, two_strip_sweeps, 0)
+    strip_sweep(strip_other, strip)
+    total = []
+    for index in range(2):
+        added = strip[index, HALO : HALO + rows]
+        added = jnp.where(lane < 64, added, pltpu.roll(added, 64, 1))
+        total.append(solved(index, everything) + added)
+    late = -(base_velocity[0] * total[0] + base_velocity[1] * total[1])
+    late = fold_late(late, 0).astype(BF16)
     late_stage[...] = late
     late_in[g] = late
     for offset in grp_offsets:
@@ -613,6 +663,10 @@
             pltpu.VMEM((2, 2, wide, LANES), F32),
             pltpu.VMEM((2, 2, wide + 2 * HALO, LANES), F32),
             pltpu.VMEM((2, 2, wide + 2 * HALO, LANES), F32),
+            pltpu.VMEM((10, wide, LANES), F32),
+            pltpu.VMEM((2, wide, LANES), F32),
+            pltpu.VMEM((2, wide + 2 * HALO, LANES), F32),
+            pltpu.VMEM((2, wide + 2 * HALO, LANES), F32),
             pltpu.VMEM((2, wide, LANES), F32),
             pltpu.VMEM((32, LANES), F32),
             pltpu.VMEM((32, LANES), F32),

time: 47.9 us -> 47.6 us (level)
  no operation moved by 1% of the time
where the time goes in v6:
time: 47.6 us; the launch traced here: 47.5 us
  Pallas kernels  46.9 us (99%)
  between operations  0.64 us (1%)
    pallas_call x1, Pallas kernels, on_device(): pl.pallas_call(functools.partial(kernel, n_grp, n_tile), out_shape=(pltpu...  46.2 us

profile of v6, /device:TPU:1, one launch (start us, length us, event | category | flops | bytes accessed | tf_op | source)
XLA Modules:
  0.0 47.5 jit_solution(11328478780323520679)
XLA Ops:
  0.6 46.2 %shard_map.112 = (f32[2,64,128]{2,1,0:T(8,128)S(1)}, f32[64,128]{1,0:T(8,128)S(1)}, f32[1,128]{1,0:T(1,128)S(1)}) custom-call(f32[2,64,128]{2,1,0:T(8,128)} %base_velocity_in.1, f32[64,128]{1,0:T(8,128)} %viscosity_in.1, f32[64,128]{1,0:T(8,128)} %friction_in.1, f32[64,128]{1,0:T(8,128)} %friction_probe_in.1, f32[1,1,2,2048]{3,2,1,0:T(2,128)} %pixel_los_in.1, ...), custom_call_target="tpu_custom_call" | custom-call | tf_op jit(solution)/shard_map/pallas_call | solution.py:638
  46.8 0.7 %shard_map.113 = (f32[2,64,128]{2,1,0:T(8,128)}, f32[64,128]{1,0:T(8,128)}, f32[1,128]{1,0:T(1,128)}) custom-call(f32[2,64,128]{2,1,0:T(8,128)S(1)} %get-tuple-element.9.a, f32[64,128]{1,0:T(8,128)S(1)} %get-tuple-element.10.b, f32[1,128]{1,0:T(1,128)S(1)} %get-tuple-element.11.c), custom_call_target="tpu_custom_call" | custom-call | tf_op jit(solution)/shard_map/pallas_call | solution.py:715
